TPU v7x, 32 devices: a whole 2x2x4 slice. The times are simulated.
32 devices in a mesh: dom: 8 (over z, x), slab: 4 (over y, core).
Axes of the slice: x: 2, y: 2, z: 4, core: 2. Of those that a mesh axis runs over, the one named last changes fastest.
Arguments:
- logperm: float32 [32, 16, 64, 128], P('dom', 'slab'), may hold values from -4.2 to 4.2
- source: float32 [16, 64, 128], P('slab'), may hold values from -6 to 6
- observed: float32 [16, 64, 128], P('slab'), may hold values from -1.2 to 1.2
- brownian: float32 [32, 32], replicated, may hold values from -6 to 6
Outputs:
- particles_next: float32 [32, 16, 64, 128], P('dom', 'slab')
All inputs are finite; a program needn't handle non-finite values.
Results may differ from a plain program's by a relative error of at most 0.0003.
Values sent between devices are 32-bit elements; how exact they have to be, the bound alone decides.
A program may use at most 64 MiB of HBM per device.

v0:
```python
import math

import jax
import jax.numpy as jnp
from jax import lax
from jax.sharding import PartitionSpec as P

SWEEPS = 8


misfit_weight = 1000.0


def with_halo(block, sides, width):
    for axis, dim in sides:
        count = lax.axis_size(axis)
        forward = [(i, i + 1) for i in range(count - 1)]
        backward = [(target, source) for source, target in forward]
        low = lax.ppermute(
            lax.slice_in_dim(block, block.shape[dim] - width, None, axis=dim), axis, forward
        )
        high = lax.ppermute(lax.slice_in_dim(block, 0, width, axis=dim), axis, backward)
        block = jnp.concatenate([low, block, high], axis=dim)
    return block


def neighbor_sum(core, below, above, fill):
    pad_y = jnp.pad(core, ((0, 0), (0, 0), (1, 1), (0, 0)), constant_values=fill)
    pad_z = jnp.pad(core, ((0, 0), (0, 0), (0, 0), (1, 1)), constant_values=fill)
    return below + above + pad_y[:, :, :-2] + pad_y[:, :, 2:] + pad_z[..., :-2] + pad_z[..., 2:]


def grad_field(e_core, e_below, e_above, p_core, p_below, p_above, q_core, q_below, q_above):
    summed = e_below * (p_core - p_below) * (q_core - q_below) + e_above * (p_core - p_above) * (
        q_core - q_above
    )
    for dimension in (2, 3):
        padding = [(0, 0), (0, 0), (0, 0), (0, 0)]
        padding[dimension] = (1, 1)
        e_pad = jnp.pad(e_core, padding, constant_values=1.0)
        p_pad = jnp.pad(p_core, padding)
        q_pad = jnp.pad(q_core, padding)
        extent = e_core.shape[dimension]
        for offset in (0, 2):
            e_near = lax.slice_in_dim(e_pad, offset, offset + extent, axis=dimension)
            p_near = lax.slice_in_dim(p_pad, offset, offset + extent, axis=dimension)
            q_near = lax.slice_in_dim(q_pad, offset, offset + extent, axis=dimension)
            summed = summed + e_near * (p_core - p_near) * (q_core - q_near)
    return -0.5 * e_core * summed


def on_device(logperm, source, observed, brownian):
    particles, width, rows_y, depth_z = logperm.shape
    slabs = lax.axis_size("slab")
    cells = width * slabs * rows_y * depth_z
    extended = with_halo(logperm, (("slab", 1),), 1)
    e_ext = jnp.exp(0.5 * extended)
    e_core = e_ext[:, 1:-1]
    inverse = 1.0 / neighbor_sum(e_core, e_ext[:, :-2], e_ext[:, 2:], 1.0)

    def relax_rim(rhs):
        value = inverse * rhs
        for sweep_index in range(SWEEPS - 1):
            bordered = with_halo(value, (("slab", 1),), 1)
            value = inverse * (
                rhs + e_core * neighbor_sum(value, bordered[:, :-2], bordered[:, 2:], 0.0)
            )
        return value / e_core

    pressure = relax_rim(source[None])
    misfit = misfit_weight * (pressure - observed[None])
    adjoint = relax_rim(misfit)
    states = with_halo(jnp.stack([pressure, adjoint]), (("slab", 2),), 1)
    gradient = grad_field(
        e_core,
        e_ext[:, :-2],
        e_ext[:, 2:],
        pressure,
        states[0][:, :-2],
        states[0][:, 2:],
        adjoint,
        states[1][:, :-2],
        states[1][:, 2:],
    )
    g_flat = gradient.reshape(particles, -1)
    u_cells, g_cells = (
        lax.all_to_all(
            logperm.reshape(particles, -1), "dom", split_axis=1, concat_axis=0, tiled=True
        ),
        lax.all_to_all(g_flat, "dom", split_axis=1, concat_axis=0, tiled=True),
    )
    ensemble = u_cells.shape[0]
    centre = jnp.mean(u_cells, axis=0, keepdims=True)
    spread = u_cells - centre
    partial_gram = lax.dot_general(
        spread,
        g_cells,
        (((1,), (1,)), ((), ())),
        precision=lax.Precision.HIGHEST,
        preferred_element_type=jnp.float32,
    )
    gram = lax.psum(partial_gram, ("dom", "slab"))
    step_size = ensemble / (4.0 * (cells + 1))
    mixing = -(step_size / ensemble) * gram + math.sqrt(2.0 * step_size / ensemble) * brownian
    moved = (
        centre
        + 1.25 * spread
        + lax.dot_general(
            mixing,
            spread,
            (((0,), (0,)), ((), ())),
            precision=lax.Precision.HIGHEST,
            preferred_element_type=jnp.float32,
        )
    )
    returned = lax.all_to_all(moved, "dom", split_axis=0, concat_axis=1, tiled=True)
    return returned.reshape(logperm.shape)


def solution(mesh):
    return jax.shard_map(
        on_device,
        mesh=mesh,
        in_specs=(P("dom", "slab", None, None), P("slab", None, None), P("slab", None, None), P()),
        out_specs=P("dom", "slab", None, None),
        check_vma=False,
    )
```

profile of v0, /device:TPU:0, one launch (start us, length us, event | category | flops | bytes accessed | tf_op | source)
XLA Modules:
  0.0 232.8 jit_solution(12804674710687503110)
XLA Ops:
  1.0 2.4 %collective-permute-start = (f32[4,1,64,128]{3,2,1,0:T(8,128)S(1)}, f32[4,1,64,128]{3,2,1,0:T(8,128)S(1)}, u32[]{:S(2)}, u32[]{:S(2)}) collective-permute-start(f32[4,1,64,128]{3,2,1,0:T(8,128)S(1)} %get-tuple-element.41), channel_id=1, source_target_pairs={{0,1},{1,2},{2,3},{4,5},{5,6},{6,7},{8,9},{9,10},{10,11},{12,13},{... | collective-permute-start | bytes 393224 | tf_op jit(solution)/shard_map/ppermute | solution.py:19
  3.4 1.3 collective-permute-start.1
  4.7 4.1 %collective-permute-done.1 = f32[4,1,64,128]{3,2,1,0:T(8,128)S(1)} collective-permute-done((f32[4,1,64,128]{3,2,1,0:T(8,128)S(1)}, f32[4,1,64,128]{3,2,1,0:T(8,128)S(1)}, u32[]{:S(2)}, u32[]{:S(2)}) %collective-permute-start.1) | collective-permute-done | bytes 131104 | tf_op jit(solution)/shard_map/ppermute | solution.py:22
  10.4 5.5 %collective-permute-start.2 = (f32[4,1,64,128]{3,2,1,0:T(8,128)S(1)}, f32[4,1,64,128]{3,2,1,0:T(8,128)S(1)}, u32[]{:S(2)}, u32[]{:S(2)}) collective-permute-start(f32[4,1,64,128]{3,2,1,0:T(8,128)S(1)} %get-tuple-element.39), channel_id=1, source_target_pairs={{0,1},{1,2},{2,3},{4,5},{5,6},{6,7},{8,9},{9,10},{10,11},{12,13},{... | collective-permute-start | bytes 393224 | tf_op jit(solution)/shard_map/ppermute | solution.py:19
  15.9 1.3 collective-permute-start.3
  17.2 1.9 collective-permute-done.3
  19.5 5.0 %collective-permute-start.4 = (f32[4,1,64,128]{3,2,1,0:T(8,128)S(1)}, f32[4,1,64,128]{3,2,1,0:T(8,128)S(1)}, u32[]{:S(2)}, u32[]{:S(2)}) collective-permute-start(f32[4,1,64,128]{3,2,1,0:T(8,128)S(1)} %get-tuple-element.37), channel_id=1, source_target_pairs={{0,1},{1,2},{2,3},{4,5},{5,6},{6,7},{8,9},{9,10},{10,11},{12,13},{... | collective-permute-start | bytes 393224 | tf_op jit(solution)/shard_map/ppermute | solution.py:19
  24.5 1.3 collective-permute-start.5
  25.8 1.9 collective-permute-done.5
  28.1 5.0 %collective-permute-start.6 = (f32[4,1,64,128]{3,2,1,0:T(8,128)S(1)}, f32[4,1,64,128]{3,2,1,0:T(8,128)S(1)}, u32[]{:S(2)}, u32[]{:S(2)}) collective-permute-start(f32[4,1,64,128]{3,2,1,0:T(8,128)S(1)} %get-tuple-element.35), channel_id=1, source_target_pairs={{0,1},{1,2},{2,3},{4,5},{5,6},{6,7},{8,9},{9,10},{10,11},{12,13},{... | collective-permute-start | bytes 393224 | tf_op jit(solution)/shard_map/ppermute | solution.py:19
  33.1 1.3 collective-permute-start.7
  34.4 1.9 collective-permute-done.7
  36.8 5.0 %collective-permute-start.8 = (f32[4,1,64,128]{3,2,1,0:T(8,128)S(1)}, f32[4,1,64,128]{3,2,1,0:T(8,128)S(1)}, u32[]{:S(2)}, u32[]{:S(2)}) collective-permute-start(f32[4,1,64,128]{3,2,1,0:T(8,128)S(1)} %get-tuple-element.33), channel_id=1, source_target_pairs={{0,1},{1,2},{2,3},{4,5},{5,6},{6,7},{8,9},{9,10},{10,11},{12,13},{... | collective-permute-start | bytes 393224 | tf_op jit(solution)/shard_map/ppermute | solution.py:19
  41.8 1.3 collective-permute-start.9
  43.1 1.9 collective-permute-done.9
  45.4 5.0 %collective-permute-start.10 = (f32[4,1,64,128]{3,2,1,0:T(8,128)S(1)}, f32[4,1,64,128]{3,2,1,0:T(8,128)S(1)}, u32[]{:S(2)}, u32[]{:S(2)}) collective-permute-start(f32[4,1,64,128]{3,2,1,0:T(8,128)S(1)} %get-tuple-element.31), channel_id=1, source_target_pairs={{0,1},{1,2},{2,3},{4,5},{5,6},{6,7},{8,9},{9,10},{10,11},{12,13},{... | collective-permute-start | bytes 393224 | tf_op jit(solution)/shard_map/ppermute | solution.py:19
  50.4 1.3 collective-permute-start.11
  51.7 1.9 collective-permute-done.11
  54.1 5.1 %collective-permute-start.12 = (f32[4,1,64,128]{3,2,1,0:T(8,128)S(1)}, f32[4,1,64,128]{3,2,1,0:T(8,128)S(1)}, u32[]{:S(2)}, u32[]{:S(2)}) collective-permute-start(f32[4,1,64,128]{3,2,1,0:T(8,128)S(1)} %get-tuple-element.29), channel_id=1, source_target_pairs={{0,1},{1,2},{2,3},{4,5},{5,6},{6,7},{8,9},{9,10},{10,11},{12,13},{... | collective-permute-start | bytes 393224 | tf_op jit(solution)/shard_map/ppermute | solution.py:19
  59.2 1.3 collective-permute-start.13
  60.5 1.9 collective-permute-done.13
  62.8 5.0 %collective-permute-start.14 = (f32[4,1,64,128]{3,2,1,0:T(8,128)S(1)}, f32[4,1,64,128]{3,2,1,0:T(8,128)S(1)}, u32[]{:S(2)}, u32[]{:S(2)}) collective-permute-start(f32[4,1,64,128]{3,2,1,0:T(8,128)S(1)} %get-tuple-element.27), channel_id=1, source_target_pairs={{0,1},{1,2},{2,3},{4,5},{5,6},{6,7},{8,9},{9,10},{10,11},{12,13},{... | collective-permute-start | bytes 393224 | tf_op jit(solution)/shard_map/ppermute | solution.py:19
  67.8 1.3 collective-permute-start.15
  69.1 1.9 collective-permute-done.15
  71.5 5.0 %collective-permute-start.16 = (f32[4,1,64,128]{3,2,1,0:T(8,128)S(1)}, f32[4,1,64,128]{3,2,1,0:T(8,128)S(1)}, u32[]{:S(2)}, u32[]{:S(2)}) collective-permute-start(f32[4,1,64,128]{3,2,1,0:T(8,128)S(1)} %get-tuple-element.25), channel_id=1, source_target_pairs={{0,1},{1,2},{2,3},{4,5},{5,6},{6,7},{8,9},{9,10},{10,11},{12,13},{... | collective-permute-start | bytes 393224 | tf_op jit(solution)/shard_map/ppermute | solution.py:19
  77.8 1.9 collective-permute-done.17
  80.2 5.0 %collective-permute-start.18 = (f32[4,1,64,128]{3,2,1,0:T(8,128)S(1)}, f32[4,1,64,128]{3,2,1,0:T(8,128)S(1)}, u32[]{:S(2)}, u32[]{:S(2)}) collective-permute-start(f32[4,1,64,128]{3,2,1,0:T(8,128)S(1)} %get-tuple-element.23), channel_id=1, source_target_pairs={{0,1},{1,2},{2,3},{4,5},{5,6},{6,7},{8,9},{9,10},{10,11},{12,13},{... | collective-permute-start | bytes 393224 | tf_op jit(solution)/shard_map/ppermute | solution.py:19
  86.5 1.9 collective-permute-done.19
  88.9 5.0 %collective-permute-start.20 = (f32[4,1,64,128]{3,2,1,0:T(8,128)S(1)}, f32[4,1,64,128]{3,2,1,0:T(8,128)S(1)}, u32[]{:S(2)}, u32[]{:S(2)}) collective-permute-start(f32[4,1,64,128]{3,2,1,0:T(8,128)S(1)} %get-tuple-element.21), channel_id=1, source_target_pairs={{0,1},{1,2},{2,3},{4,5},{5,6},{6,7},{8,9},{9,10},{10,11},{12,13},{... | collective-permute-start | bytes 393224 | tf_op jit(solution)/shard_map/ppermute | solution.py:19
  95.2 1.9 collective-permute-done.21
  97.6 5.0 %collective-permute-start.22 = (f32[4,1,64,128]{3,2,1,0:T(8,128)S(1)}, f32[4,1,64,128]{3,2,1,0:T(8,128)S(1)}, u32[]{:S(2)}, u32[]{:S(2)}) collective-permute-start(f32[4,1,64,128]{3,2,1,0:T(8,128)S(1)} %get-tuple-element.19), channel_id=1, source_target_pairs={{0,1},{1,2},{2,3},{4,5},{5,6},{6,7},{8,9},{9,10},{10,11},{12,13},{... | collective-permute-start | bytes 393224 | tf_op jit(solution)/shard_map/ppermute | solution.py:19
  103.9 1.9 collective-permute-done.23
  106.3 5.0 %collective-permute-start.24 = (f32[4,1,64,128]{3,2,1,0:T(8,128)S(1)}, f32[4,1,64,128]{3,2,1,0:T(8,128)S(1)}, u32[]{:S(2)}, u32[]{:S(2)}) collective-permute-start(f32[4,1,64,128]{3,2,1,0:T(8,128)S(1)} %get-tuple-element.17), channel_id=1, source_target_pairs={{0,1},{1,2},{2,3},{4,5},{5,6},{6,7},{8,9},{9,10},{10,11},{12,13},{... | collective-permute-start | bytes 393224 | tf_op jit(solution)/shard_map/ppermute | solution.py:19
  111.3 1.4 collective-permute-start.25
  112.7 1.9 collective-permute-done.25
  115.9 5.6 %collective-permute-start.26 = (f32[4,1,64,128]{3,2,1,0:T(8,128)}, f32[4,1,64,128]{3,2,1,0:T(8,128)}, u32[]{:S(2)}, u32[]{:S(2)}) collective-permute-start(f32[4,1,64,128]{3,2,1,0:T(8,128)} %get-tuple-element.15), channel_id=1, source_target_pairs={{0,1},{1,2},{2,3},{4,5},{5,6},{6,7},{8,9},{9,10},{10,11},{12,13},{... | collective-permute-start | bytes 393224 | tf_op jit(solution)/shard_map/ppermute | solution.py:19
  123.6 2.2 copy.7
  125.8 5.8 %all-to-all-start = ((f32[4,8,4096]{2,0,1:T(4,128)}), f32[4,8,4096]{2,0,1:T(4,128)S(1)}, u32[]{:S(2)}, u32[]{:S(2)}) async-start(f32[4,8,4096]{2,0,1:T(4,128)} %copy.7), calls=%async_computation | async-start | bytes 1048576 | tf_op jit(solution)/shard_map/all_to_all | solution.py:87
  131.6 1.3 fusion.92
  133.0 2.8 %collective-permute-start.28 = (f32[4,1,64,128]{3,2,1,0:T(8,128)S(1)}, f32[4,1,64,128]{3,2,1,0:T(8,128)S(1)}, u32[]{:S(2)}, u32[]{:S(2)}) collective-permute-start(f32[4,1,64,128]{3,2,1,0:T(8,128)S(1)} %get-tuple-element.13), channel_id=1, source_target_pairs={{0,1},{1,2},{2,3},{4,5},{5,6},{6,7},{8,9},{9,10},{10,11},{12,13},{... | collective-permute-start | bytes 393224 | tf_op jit(solution)/shard_map/ppermute | solution.py:19
  137.1 2.3 %collective-permute-done.29 = f32[4,1,64,128]{3,2,1,0:T(8,128)S(1)} collective-permute-done((f32[4,1,64,128]{3,2,1,0:T(8,128)S(1)}, f32[4,1,64,128]{3,2,1,0:T(8,128)S(1)}, u32[]{:S(2)}, u32[]{:S(2)}) %collective-permute-start.29) | collective-permute-done | bytes 131104 | tf_op jit(solution)/shard_map/ppermute | solution.py:22
  140.7 5.7 %collective-permute-start.30 = (f32[2,4,1,64,128]{4,3,2,1,0:T(8,128)}, f32[2,4,1,64,128]{4,3,2,1,0:T(8,128)S(1)}, u32[]{:S(2)}, u32[]{:S(2)}) collective-permute-start(f32[2,4,1,64,128]{4,3,2,1,0:T(8,128)} %get-tuple-element.11), channel_id=1, source_target_pairs={{0,1},{1,2},{2,3},{4,5},{5,6},{6,7},{8,9},{9,10},{10,11},{12,13},{... | collective-permute-start | bytes 786440 | tf_op jit(solution)/shard_map/ppermute | solution.py:19
  146.5 1.3 collective-permute-start.31
  147.9 2.2 collective-permute-done.31
  152.7 6.0 %all-to-all-start.1 = ((f32[4,8,4096]{2,0,1:T(4,128)}), f32[4,8,4096]{2,0,1:T(4,128)S(1)}, u32[]{:S(2)}, u32[]{:S(2)}) async-start(f32[4,8,4096]{2,0,1:T(4,128)} %copy.8), calls=%async_computation.1 | async-start | bytes 1048576 | tf_op jit(solution)/shard_map/all_to_all | solution.py:90
  159.2 11.0 %all-to-all-done.1 = f32[4,8,4096]{2,0,1:T(4,128)S(1)} async-done(((f32[4,8,4096]{2,0,1:T(4,128)}), f32[4,8,4096]{2,0,1:T(4,128)S(1)}, u32[]{:S(2)}, u32[]{:S(2)}) %all-to-all-start.1) | async-done | bytes 524320 | tf_op jit(solution)/shard_map/all_to_all | solution.py:90
  170.9 40.8 %psum.7 = f32[32,32]{1,0:T(8,128)S(1)} all-reduce(f32[32,32]{1,0:T(8,128)S(1)} %fusion.167), channel_id=1, replica_groups=mesh['dom'=8,'slab'=4] {'dom','slab'}, use_global_device_ids=true, to_apply=%region_1.2 | all-reduce | flops 1024 | bytes 8192 | tf_op jit(solution)/shard_map/psum | solution.py:102
  212.6 19.0 %all_to_all.54 = f32[8,4,4096]{2,1,0:T(4,128)S(1)} all-to-all(f32[8,4,4096]{2,1,0:T(4,128)S(1)} %all_to_all.48), channel_id=1, replica_groups=mesh['dom'=8,'slab'=4] {'dom'}, dimensions={0} | all-to-all | bytes 1048576 | tf_op jit(solution)/shard_map/all_to_all | solution.py:116
  (81 shorter events, 24.4 us)
Async XLA Ops:
  0.0 10.0 %copy-start.1 = (f32[4,64,128]{2,1,0:T(8,128)S(1)}, f32[4,64,128]{2,1,0:T(8,128)}, u32[]{:S(2)}) copy-start(f32[4,64,128]{2,1,0:T(8,128)} %param.5) | copy-start | bytes 393220
  1.0 3.7 %collective-permute-start = (f32[4,1,64,128]{3,2,1,0:T(8,128)S(1)}, f32[4,1,64,128]{3,2,1,0:T(8,128)S(1)}, u32[]{:S(2)}, u32[]{:S(2)}) collective-permute-start(f32[4,1,64,128]{3,2,1,0:T(8,128)S(1)} %get-tuple-element.41), channel_id=1, source_target_pairs={{0,1},{1,2},{2,3},{4,5},{5,6},{6,7},{8,9},{9,10},{10,11},{12,13},{... | collective-permute-start | bytes 393224 | tf_op jit(solution)/shard_map/ppermute | solution.py:19
  3.4 5.4 %collective-permute-start.1 = (f32[4,1,64,128]{3,2,1,0:T(8,128)S(1)}, f32[4,1,64,128]{3,2,1,0:T(8,128)S(1)}, u32[]{:S(2)}, u32[]{:S(2)}) collective-permute-start(f32[4,1,64,128]{3,2,1,0:T(8,128)S(1)} %get-tuple-element.42), channel_id=1, source_target_pairs={{1,0},{2,1},{3,2},{5,4},{6,5},{7,6},{9,8},{10,9},{11,10},{13,12},{... | collective-permute-start | bytes 393224 | tf_op jit(solution)/shard_map/ppermute | solution.py:22
  10.4 6.8 %collective-permute-start.2 = (f32[4,1,64,128]{3,2,1,0:T(8,128)S(1)}, f32[4,1,64,128]{3,2,1,0:T(8,128)S(1)}, u32[]{:S(2)}, u32[]{:S(2)}) collective-permute-start(f32[4,1,64,128]{3,2,1,0:T(8,128)S(1)} %get-tuple-element.39), channel_id=1, source_target_pairs={{0,1},{1,2},{2,3},{4,5},{5,6},{6,7},{8,9},{9,10},{10,11},{12,13},{... | collective-permute-start | bytes 393224 | tf_op jit(solution)/shard_map/ppermute | solution.py:19
  15.9 3.2 %collective-permute-start.3 = (f32[4,1,64,128]{3,2,1,0:T(8,128)S(1)}, f32[4,1,64,128]{3,2,1,0:T(8,128)S(1)}, u32[]{:S(2)}, u32[]{:S(2)}) collective-permute-start(f32[4,1,64,128]{3,2,1,0:T(8,128)S(1)} %get-tuple-element.40), channel_id=1, source_target_pairs={{1,0},{2,1},{3,2},{5,4},{6,5},{7,6},{9,8},{10,9},{11,10},{13,12},{... | collective-permute-start | bytes 393224 | tf_op jit(solution)/shard_map/ppermute | solution.py:22
  19.5 6.3 %collective-permute-start.4 = (f32[4,1,64,128]{3,2,1,0:T(8,128)S(1)}, f32[4,1,64,128]{3,2,1,0:T(8,128)S(1)}, u32[]{:S(2)}, u32[]{:S(2)}) collective-permute-start(f32[4,1,64,128]{3,2,1,0:T(8,128)S(1)} %get-tuple-element.37), channel_id=1, source_target_pairs={{0,1},{1,2},{2,3},{4,5},{5,6},{6,7},{8,9},{9,10},{10,11},{12,13},{... | collective-permute-start | bytes 393224 | tf_op jit(solution)/shard_map/ppermute | solution.py:19
  24.5 3.2 %collective-permute-start.5 = (f32[4,1,64,128]{3,2,1,0:T(8,128)S(1)}, f32[4,1,64,128]{3,2,1,0:T(8,128)S(1)}, u32[]{:S(2)}, u32[]{:S(2)}) collective-permute-start(f32[4,1,64,128]{3,2,1,0:T(8,128)S(1)} %get-tuple-element.38), channel_id=1, source_target_pairs={{1,0},{2,1},{3,2},{5,4},{6,5},{7,6},{9,8},{10,9},{11,10},{13,12},{... | collective-permute-start | bytes 393224 | tf_op jit(solution)/shard_map/ppermute | solution.py:22
  28.1 6.3 %collective-permute-start.6 = (f32[4,1,64,128]{3,2,1,0:T(8,128)S(1)}, f32[4,1,64,128]{3,2,1,0:T(8,128)S(1)}, u32[]{:S(2)}, u32[]{:S(2)}) collective-permute-start(f32[4,1,64,128]{3,2,1,0:T(8,128)S(1)} %get-tuple-element.35), channel_id=1, source_target_pairs={{0,1},{1,2},{2,3},{4,5},{5,6},{6,7},{8,9},{9,10},{10,11},{12,13},{... | collective-permute-start | bytes 393224 | tf_op jit(solution)/shard_map/ppermute | solution.py:19
  33.1 3.2 %collective-permute-start.7 = (f32[4,1,64,128]{3,2,1,0:T(8,128)S(1)}, f32[4,1,64,128]{3,2,1,0:T(8,128)S(1)}, u32[]{:S(2)}, u32[]{:S(2)}) collective-permute-start(f32[4,1,64,128]{3,2,1,0:T(8,128)S(1)} %get-tuple-element.36), channel_id=1, source_target_pairs={{1,0},{2,1},{3,2},{5,4},{6,5},{7,6},{9,8},{10,9},{11,10},{13,12},{... | collective-permute-start | bytes 393224 | tf_op jit(solution)/shard_map/ppermute | solution.py:22
  36.8 6.3 %collective-permute-start.8 = (f32[4,1,64,128]{3,2,1,0:T(8,128)S(1)}, f32[4,1,64,128]{3,2,1,0:T(8,128)S(1)}, u32[]{:S(2)}, u32[]{:S(2)}) collective-permute-start(f32[4,1,64,128]{3,2,1,0:T(8,128)S(1)} %get-tuple-element.33), channel_id=1, source_target_pairs={{0,1},{1,2},{2,3},{4,5},{5,6},{6,7},{8,9},{9,10},{10,11},{12,13},{... | collective-permute-start | bytes 393224 | tf_op jit(solution)/shard_map/ppermute | solution.py:19
  41.8 3.2 %collective-permute-start.9 = (f32[4,1,64,128]{3,2,1,0:T(8,128)S(1)}, f32[4,1,64,128]{3,2,1,0:T(8,128)S(1)}, u32[]{:S(2)}, u32[]{:S(2)}) collective-permute-start(f32[4,1,64,128]{3,2,1,0:T(8,128)S(1)} %get-tuple-element.34), channel_id=1, source_target_pairs={{1,0},{2,1},{3,2},{5,4},{6,5},{7,6},{9,8},{10,9},{11,10},{13,12},{... | collective-permute-start | bytes 393224 | tf_op jit(solution)/shard_map/ppermute | solution.py:22
  45.4 6.3 %collective-permute-start.10 = (f32[4,1,64,128]{3,2,1,0:T(8,128)S(1)}, f32[4,1,64,128]{3,2,1,0:T(8,128)S(1)}, u32[]{:S(2)}, u32[]{:S(2)}) collective-permute-start(f32[4,1,64,128]{3,2,1,0:T(8,128)S(1)} %get-tuple-element.31), channel_id=1, source_target_pairs={{0,1},{1,2},{2,3},{4,5},{5,6},{6,7},{8,9},{9,10},{10,11},{12,13},{... | collective-permute-start | bytes 393224 | tf_op jit(solution)/shard_map/ppermute | solution.py:19
  50.4 3.2 %collective-permute-start.11 = (f32[4,1,64,128]{3,2,1,0:T(8,128)S(1)}, f32[4,1,64,128]{3,2,1,0:T(8,128)S(1)}, u32[]{:S(2)}, u32[]{:S(2)}) collective-permute-start(f32[4,1,64,128]{3,2,1,0:T(8,128)S(1)} %get-tuple-element.32), channel_id=1, source_target_pairs={{1,0},{2,1},{3,2},{5,4},{6,5},{7,6},{9,8},{10,9},{11,10},{13,12},{... | collective-permute-start | bytes 393224 | tf_op jit(solution)/shard_map/ppermute | solution.py:22
  54.0 17.0 %copy-start = (f32[4,64,128]{2,1,0:T(8,128)S(1)}, f32[4,64,128]{2,1,0:T(8,128)}, u32[]{:S(2)}) copy-start(f32[4,64,128]{2,1,0:T(8,128)} %param.6) | copy-start | bytes 393220
  54.1 6.4 %collective-permute-start.12 = (f32[4,1,64,128]{3,2,1,0:T(8,128)S(1)}, f32[4,1,64,128]{3,2,1,0:T(8,128)S(1)}, u32[]{:S(2)}, u32[]{:S(2)}) collective-permute-start(f32[4,1,64,128]{3,2,1,0:T(8,128)S(1)} %get-tuple-element.29), channel_id=1, source_target_pairs={{0,1},{1,2},{2,3},{4,5},{5,6},{6,7},{8,9},{9,10},{10,11},{12,13},{... | collective-permute-start | bytes 393224 | tf_op jit(solution)/shard_map/ppermute | solution.py:19
  59.2 3.2 %collective-permute-start.13 = (f32[4,1,64,128]{3,2,1,0:T(8,128)S(1)}, f32[4,1,64,128]{3,2,1,0:T(8,128)S(1)}, u32[]{:S(2)}, u32[]{:S(2)}) collective-permute-start(f32[4,1,64,128]{3,2,1,0:T(8,128)S(1)} %get-tuple-element.30), channel_id=1, source_target_pairs={{1,0},{2,1},{3,2},{5,4},{6,5},{7,6},{9,8},{10,9},{11,10},{13,12},{... | collective-permute-start | bytes 393224 | tf_op jit(solution)/shard_map/ppermute | solution.py:22
  62.8 6.3 %collective-permute-start.14 = (f32[4,1,64,128]{3,2,1,0:T(8,128)S(1)}, f32[4,1,64,128]{3,2,1,0:T(8,128)S(1)}, u32[]{:S(2)}, u32[]{:S(2)}) collective-permute-start(f32[4,1,64,128]{3,2,1,0:T(8,128)S(1)} %get-tuple-element.27), channel_id=1, source_target_pairs={{0,1},{1,2},{2,3},{4,5},{5,6},{6,7},{8,9},{9,10},{10,11},{12,13},{... | collective-permute-start | bytes 393224 | tf_op jit(solution)/shard_map/ppermute | solution.py:19
  67.8 3.2 %collective-permute-start.15 = (f32[4,1,64,128]{3,2,1,0:T(8,128)S(1)}, f32[4,1,64,128]{3,2,1,0:T(8,128)S(1)}, u32[]{:S(2)}, u32[]{:S(2)}) collective-permute-start(f32[4,1,64,128]{3,2,1,0:T(8,128)S(1)} %get-tuple-element.28), channel_id=1, source_target_pairs={{1,0},{2,1},{3,2},{5,4},{6,5},{7,6},{9,8},{10,9},{11,10},{13,12},{... | collective-permute-start | bytes 393224 | tf_op jit(solution)/shard_map/ppermute | solution.py:22
  71.5 6.3 %collective-permute-start.16 = (f32[4,1,64,128]{3,2,1,0:T(8,128)S(1)}, f32[4,1,64,128]{3,2,1,0:T(8,128)S(1)}, u32[]{:S(2)}, u32[]{:S(2)}) collective-permute-start(f32[4,1,64,128]{3,2,1,0:T(8,128)S(1)} %get-tuple-element.25), channel_id=1, source_target_pairs={{0,1},{1,2},{2,3},{4,5},{5,6},{6,7},{8,9},{9,10},{10,11},{12,13},{... | collective-permute-start | bytes 393224 | tf_op jit(solution)/shard_map/ppermute | solution.py:19
  76.5 3.2 %collective-permute-start.17 = (f32[4,1,64,128]{3,2,1,0:T(8,128)S(1)}, f32[4,1,64,128]{3,2,1,0:T(8,128)S(1)}, u32[]{:S(2)}, u32[]{:S(2)}) collective-permute-start(f32[4,1,64,128]{3,2,1,0:T(8,128)S(1)} %get-tuple-element.26), channel_id=1, source_target_pairs={{1,0},{2,1},{3,2},{5,4},{6,5},{7,6},{9,8},{10,9},{11,10},{13,12},{... | collective-permute-start | bytes 393224 | tf_op jit(solution)/shard_map/ppermute | solution.py:22
  80.2 6.3 %collective-permute-start.18 = (f32[4,1,64,128]{3,2,1,0:T(8,128)S(1)}, f32[4,1,64,128]{3,2,1,0:T(8,128)S(1)}, u32[]{:S(2)}, u32[]{:S(2)}) collective-permute-start(f32[4,1,64,128]{3,2,1,0:T(8,128)S(1)} %get-tuple-element.23), channel_id=1, source_target_pairs={{0,1},{1,2},{2,3},{4,5},{5,6},{6,7},{8,9},{9,10},{10,11},{12,13},{... | collective-permute-start | bytes 393224 | tf_op jit(solution)/shard_map/ppermute | solution.py:19
  85.2 3.2 %collective-permute-start.19 = (f32[4,1,64,128]{3,2,1,0:T(8,128)S(1)}, f32[4,1,64,128]{3,2,1,0:T(8,128)S(1)}, u32[]{:S(2)}, u32[]{:S(2)}) collective-permute-start(f32[4,1,64,128]{3,2,1,0:T(8,128)S(1)} %get-tuple-element.24), channel_id=1, source_target_pairs={{1,0},{2,1},{3,2},{5,4},{6,5},{7,6},{9,8},{10,9},{11,10},{13,12},{... | collective-permute-start | bytes 393224 | tf_op jit(solution)/shard_map/ppermute | solution.py:22
  88.9 6.3 %collective-permute-start.20 = (f32[4,1,64,128]{3,2,1,0:T(8,128)S(1)}, f32[4,1,64,128]{3,2,1,0:T(8,128)S(1)}, u32[]{:S(2)}, u32[]{:S(2)}) collective-permute-start(f32[4,1,64,128]{3,2,1,0:T(8,128)S(1)} %get-tuple-element.21), channel_id=1, source_target_pairs={{0,1},{1,2},{2,3},{4,5},{5,6},{6,7},{8,9},{9,10},{10,11},{12,13},{... | collective-permute-start | bytes 393224 | tf_op jit(solution)/shard_map/ppermute | solution.py:19
  93.9 3.2 %collective-permute-start.21 = (f32[4,1,64,128]{3,2,1,0:T(8,128)S(1)}, f32[4,1,64,128]{3,2,1,0:T(8,128)S(1)}, u32[]{:S(2)}, u32[]{:S(2)}) collective-permute-start(f32[4,1,64,128]{3,2,1,0:T(8,128)S(1)} %get-tuple-element.22), channel_id=1, source_target_pairs={{1,0},{2,1},{3,2},{5,4},{6,5},{7,6},{9,8},{10,9},{11,10},{13,12},{... | collective-permute-start | bytes 393224 | tf_op jit(solution)/shard_map/ppermute | solution.py:22
  97.6 6.3 %collective-permute-start.22 = (f32[4,1,64,128]{3,2,1,0:T(8,128)S(1)}, f32[4,1,64,128]{3,2,1,0:T(8,128)S(1)}, u32[]{:S(2)}, u32[]{:S(2)}) collective-permute-start(f32[4,1,64,128]{3,2,1,0:T(8,128)S(1)} %get-tuple-element.19), channel_id=1, source_target_pairs={{0,1},{1,2},{2,3},{4,5},{5,6},{6,7},{8,9},{9,10},{10,11},{12,13},{... | collective-permute-start | bytes 393224 | tf_op jit(solution)/shard_map/ppermute | solution.py:19
  102.6 3.2 %collective-permute-start.23 = (f32[4,1,64,128]{3,2,1,0:T(8,128)S(1)}, f32[4,1,64,128]{3,2,1,0:T(8,128)S(1)}, u32[]{:S(2)}, u32[]{:S(2)}) collective-permute-start(f32[4,1,64,128]{3,2,1,0:T(8,128)S(1)} %get-tuple-element.20), channel_id=1, source_target_pairs={{1,0},{2,1},{3,2},{5,4},{6,5},{7,6},{9,8},{10,9},{11,10},{13,12},{... | collective-permute-start | bytes 393224 | tf_op jit(solution)/shard_map/ppermute | solution.py:22
  106.3 6.4 %collective-permute-start.24 = (f32[4,1,64,128]{3,2,1,0:T(8,128)S(1)}, f32[4,1,64,128]{3,2,1,0:T(8,128)S(1)}, u32[]{:S(2)}, u32[]{:S(2)}) collective-permute-start(f32[4,1,64,128]{3,2,1,0:T(8,128)S(1)} %get-tuple-element.17), channel_id=1, source_target_pairs={{0,1},{1,2},{2,3},{4,5},{5,6},{6,7},{8,9},{9,10},{10,11},{12,13},{... | collective-permute-start | bytes 393224 | tf_op jit(solution)/shard_map/ppermute | solution.py:19
  111.3 11.5 %copy-start.2 = (f32[4,4,64,128]{3,2,1,0:T(8,128)S(1)}, f32[4,4,64,128]{3,2,1,0:T(8,128)}, u32[]{:S(2)}) copy-start(f32[4,4,64,128]{3,2,1,0:T(8,128)} %param.4) | copy-start | bytes 1572868
  111.3 3.4 %collective-permute-start.25 = (f32[4,1,64,128]{3,2,1,0:T(8,128)S(1)}, f32[4,1,64,128]{3,2,1,0:T(8,128)S(1)}, u32[]{:S(2)}, u32[]{:S(2)}) collective-permute-start(f32[4,1,64,128]{3,2,1,0:T(8,128)S(1)} %get-tuple-element.18), channel_id=1, source_target_pairs={{1,0},{2,1},{3,2},{5,4},{6,5},{7,6},{9,8},{10,9},{11,10},{13,12},{... | collective-permute-start | bytes 393224 | tf_op jit(solution)/shard_map/ppermute | solution.py:22
  115.9 15.8 %collective-permute-start.26 = (f32[4,1,64,128]{3,2,1,0:T(8,128)}, f32[4,1,64,128]{3,2,1,0:T(8,128)}, u32[]{:S(2)}, u32[]{:S(2)}) collective-permute-start(f32[4,1,64,128]{3,2,1,0:T(8,128)} %get-tuple-element.15), channel_id=1, source_target_pairs={{0,1},{1,2},{2,3},{4,5},{5,6},{6,7},{8,9},{9,10},{10,11},{12,13},{... | collective-permute-start | bytes 393224 | tf_op jit(solution)/shard_map/ppermute | solution.py:19
  121.5 10.2 %collective-permute-start.27 = (f32[4,1,64,128]{3,2,1,0:T(8,128)}, f32[4,1,64,128]{3,2,1,0:T(8,128)}, u32[]{:S(2)}, u32[]{:S(2)}) collective-permute-start(f32[4,1,64,128]{3,2,1,0:T(8,128)} %get-tuple-element.16), channel_id=1, source_target_pairs={{1,0},{2,1},{3,2},{5,4},{6,5},{7,6},{9,8},{10,9},{11,10},{13,12},{... | collective-permute-start | bytes 393224 | tf_op jit(solution)/shard_map/ppermute | solution.py:22
  125.8 22.0 %all-to-all-start = ((f32[4,8,4096]{2,0,1:T(4,128)}), f32[4,8,4096]{2,0,1:T(4,128)S(1)}, u32[]{:S(2)}, u32[]{:S(2)}) async-start(f32[4,8,4096]{2,0,1:T(4,128)} %copy.7), calls=%async_computation | async-start | bytes 1048576 | tf_op jit(solution)/shard_map/all_to_all | solution.py:87
  133.0 4.1 %collective-permute-start.28 = (f32[4,1,64,128]{3,2,1,0:T(8,128)S(1)}, f32[4,1,64,128]{3,2,1,0:T(8,128)S(1)}, u32[]{:S(2)}, u32[]{:S(2)}) collective-permute-start(f32[4,1,64,128]{3,2,1,0:T(8,128)S(1)} %get-tuple-element.13), channel_id=1, source_target_pairs={{0,1},{1,2},{2,3},{4,5},{5,6},{6,7},{8,9},{9,10},{10,11},{12,13},{... | collective-permute-start | bytes 393224 | tf_op jit(solution)/shard_map/ppermute | solution.py:19
  135.8 3.6 %collective-permute-start.29 = (f32[4,1,64,128]{3,2,1,0:T(8,128)S(1)}, f32[4,1,64,128]{3,2,1,0:T(8,128)S(1)}, u32[]{:S(2)}, u32[]{:S(2)}) collective-permute-start(f32[4,1,64,128]{3,2,1,0:T(8,128)S(1)} %get-tuple-element.14), channel_id=1, source_target_pairs={{1,0},{2,1},{3,2},{5,4},{6,5},{7,6},{9,8},{10,9},{11,10},{13,12},{... | collective-permute-start | bytes 393224 | tf_op jit(solution)/shard_map/ppermute | solution.py:22
  140.7 7.2 %collective-permute-start.30 = (f32[2,4,1,64,128]{4,3,2,1,0:T(8,128)}, f32[2,4,1,64,128]{4,3,2,1,0:T(8,128)S(1)}, u32[]{:S(2)}, u32[]{:S(2)}) collective-permute-start(f32[2,4,1,64,128]{4,3,2,1,0:T(8,128)} %get-tuple-element.11), channel_id=1, source_target_pairs={{0,1},{1,2},{2,3},{4,5},{5,6},{6,7},{8,9},{9,10},{10,11},{12,13},{... | collective-permute-start | bytes 786440 | tf_op jit(solution)/shard_map/ppermute | solution.py:19
  146.5 3.6 %collective-permute-start.31 = (f32[2,4,1,64,128]{4,3,2,1,0:T(8,128)}, f32[2,4,1,64,128]{4,3,2,1,0:T(8,128)S(1)}, u32[]{:S(2)}, u32[]{:S(2)}) collective-permute-start(f32[2,4,1,64,128]{4,3,2,1,0:T(8,128)} %get-tuple-element.12), channel_id=1, source_target_pairs={{1,0},{2,1},{3,2},{5,4},{6,5},{7,6},{9,8},{10,9},{11,10},{13,12},{... | collective-permute-start | bytes 786440 | tf_op jit(solution)/shard_map/ppermute | solution.py:22
  152.7 17.5 %all-to-all-start.1 = ((f32[4,8,4096]{2,0,1:T(4,128)}), f32[4,8,4096]{2,0,1:T(4,128)S(1)}, u32[]{:S(2)}, u32[]{:S(2)}) async-start(f32[4,8,4096]{2,0,1:T(4,128)} %copy.8), calls=%async_computation.1 | async-start | bytes 1048576 | tf_op jit(solution)/shard_map/all_to_all | solution.py:90
  159.0 52.7 %copy-start.3 = (f32[32,32]{1,0:T(8,128)S(1)}, f32[32,32]{1,0:T(8,128)}, u32[]{:S(2)}) copy-start(f32[32,32]{1,0:T(8,128)} %param.7) | copy-start | bytes 12292
where the time goes:
time: 234 us; the launch traced here: 233 us
  starting transfers between devices  109 us (47%)
  blocking collectives  59.9 us (26%)
  waiting for transfers between devices  42.8 us (18%)
  other arithmetic  10.5 us (4%)
  local copies, waits for them, and re-layouts  8.39 us (4%)
    ppermute x16, starting transfers between devices, with_halo(): lax.ppermute(lax.slice_in_dim(block, block.shape[dim] - width, None, axis...  76.6 us
    psum x1, blocking collectives, on_device(): gram = lax.psum(partial_gram, ('dom', 'slab'))  40.8 us
    ppermute x16, waiting for transfers between devices, with_halo(): lax.ppermute(lax.slice_in_dim(block, 0, width, axis=dim), axis, backward)  31.8 us
    ppermute x16, starting transfers between devices, with_halo(): lax.ppermute(lax.slice_in_dim(block, 0, width, axis=dim), axis, backward)  20.8 us
    all_to_all x1, blocking collectives, on_device(): lax.all_to_all(moved, 'dom', split_axis=0, concat_axis=1, tiled=True)  19 us
    all_to_all x1, waiting for transfers between devices, on_device(): lax.all_to_all(g_flat, 'dom', split_axis=1, concat_axis=0, tiled=True)  11 us
    all_to_all x1, starting transfers between devices, on_device(): lax.all_to_all(g_flat, 'dom', split_axis=1, concat_axis=0, tiled=True)  6.02 us
    mul x12, other arithmetic, relax_rim(): inverse * (rhs + e_core * neighbor_sum(value, bordered[:, :-2], bordered[...  5.86 us
  transfers between devices with their start and end apart: 34, of which 16 were waited for; matrix products, arithmetic and copies ran while one was open for 2% of the time, Pallas kernels for 0%

commit v1 on v0

v1 whole, which is shorter than its diff:
```python
import math

import jax
import jax.numpy as jnp
from jax import lax
from jax.experimental import pallas as pl
from jax.experimental.pallas import tpu as pltpu
from jax.sharding import PartitionSpec as P

SWEEPS = 8
misfit_weight = 1000.0
VMEM_BYTES = 48 * 1024 * 1024
TOP = 8


def lane_masks(shape):
    lane = lax.broadcasted_iota(jnp.int32, shape, len(shape) - 1)
    return lane == 0, lane == shape[-1] - 1


def along_lanes(value, masks, fill):
    depth = value.shape[-1]
    before = jnp.where(masks[0], fill, pltpu.roll(value, 1, value.ndim - 1))
    after = jnp.where(masks[1], fill, pltpu.roll(value, depth - 1, value.ndim - 1))
    return before, after


def neighbors(ref, layer, rows, masks, fill):
    core = ref[layer + 1, TOP : TOP + rows]
    return core, (
        ref[layer, TOP : TOP + rows],
        ref[layer + 2, TOP : TOP + rows],
        ref[layer + 1, TOP - 1 : TOP + rows - 1],
        ref[layer + 1, TOP + 1 : TOP + rows + 1],
        *along_lanes(core, masks, fill),
    )


def border(ref, layers, rows, depth, fill):
    ref[0] = jnp.full((rows + 2 * TOP, depth), fill, jnp.float32)
    ref[layers + 1] = jnp.full((rows + 2 * TOP, depth), fill, jnp.float32)
    edge = jnp.full((layers + 2, TOP, depth), fill, jnp.float32)
    ref[:, 0:TOP] = edge
    ref[:, TOP + rows :] = edge


def scratch_fields(layers, rows, depth):
    padded = pltpu.VMEM((layers + 2, rows + 2 * TOP, depth), jnp.float32)
    plain = pltpu.VMEM((layers, rows, depth), jnp.float32)
    return [padded] * 4 + [plain] * 3


def set_borders(fields, layers, rows, depth):
    border(fields[0], layers, rows, depth, 1.0)
    for ref in fields[1:4]:
        border(ref, layers, rows, depth, 0.0)


def coefficients(logperm, fields):
    e, inverse, gain = fields[0], fields[4], fields[5]
    layers, rows, depth = inverse.shape
    masks = lane_masks((rows, depth))

    def exponent(layer, carry):
        e[layer + 1, TOP : TOP + rows] = jnp.exp(0.5 * logperm(layer))
        return carry

    lax.fori_loop(0, layers, exponent, 0)

    def divide(layer, carry):
        core, near = neighbors(e, layer, rows, masks, 1.0)
        total = 1.0 / (near[0] + near[1] + near[2] + near[3] + near[4] + near[5])
        inverse[layer] = total
        gain[layer] = core * total
        return carry

    lax.fori_loop(0, layers, divide, 0)


def relax(rhs, ping, pong, fields):
    e, inverse, gain, start = fields[0], fields[4], fields[5], fields[6]
    layers, rows, depth = inverse.shape
    masks = lane_masks((rows, depth))

    def first(layer, carry):
        value = inverse[layer] * rhs(layer)
        start[layer] = value
        ping[layer + 1, TOP : TOP + rows] = value
        return carry

    lax.fori_loop(0, layers, first, 0)

    def swept(old, layer):
        _, near = neighbors(old, layer, rows, masks, 0.0)
        total = (near[0] + near[1]) + (near[2] + near[3]) + (near[4] + near[5])
        return start[layer] + gain[layer] * total

    def sweep(old, new):
        def one(layer, carry):
            new[layer + 1, TOP : TOP + rows] = swept(old, layer)
            return carry

        lax.fori_loop(0, layers, one, 0, unroll=2)

    def pair(index, carry):
        sweep(ping, pong)
        sweep(pong, ping)
        return carry

    lax.fori_loop(0, (SWEEPS - 2) // 2, pair, 0)

    def last(layer, carry):
        pong[layer + 1, TOP : TOP + rows] = swept(ping, layer) / e[layer + 1, TOP : TOP + rows]
        return carry

    lax.fori_loop(0, layers, last, 0, unroll=2)


def gradient_layer(layer, fields):
    e, pressure, adjoint = fields[0], fields[2], fields[3]
    _, rows, depth = fields[4].shape
    masks = lane_masks((rows, depth))
    e_core, e_near = neighbors(e, layer, rows, masks, 1.0)
    p_core, p_near = neighbors(pressure, layer, rows, masks, 0.0)
    q_core, q_near = neighbors(adjoint, layer, rows, masks, 0.0)
    total = e_near[0] * (p_core - p_near[0]) * (q_core - q_near[0])
    for side in range(1, 6):
        total = total + e_near[side] * (p_core - p_near[side]) * (q_core - q_near[side])
    return -0.5 * e_core * total


def solve_kernel(logperm, source, observed, gradient, *fields):
    layers, rows, depth = gradient.shape
    set_borders(fields, layers, rows, depth)
    coefficients(lambda layer: logperm[layer], fields)
    relax(lambda layer: source[layer], fields[1], fields[2], fields)
    pressure = fields[2]

    def misfit(layer):
        return misfit_weight * (pressure[layer + 1, TOP : TOP + rows] - observed[layer])

    relax(misfit, fields[1], fields[3], fields)

    def store(layer, carry):
        gradient[layer] = gradient_layer(layer, fields)
        return carry

    lax.fori_loop(0, layers, store, 0)


def solve(logperm, source, observed):
    layers, rows, depth = logperm.shape
    return pl.pallas_call(
        solve_kernel,
        out_shape=jax.ShapeDtypeStruct(logperm.shape, jnp.float32),
        in_specs=[pl.BlockSpec(memory_space=pltpu.VMEM)] * 3,
        out_specs=pl.BlockSpec(memory_space=pltpu.VMEM),
        scratch_shapes=scratch_fields(layers, rows, depth),
        compiler_params=pltpu.CompilerParams(vmem_limit_bytes=VMEM_BYTES),
        cost_estimate=pl.CostEstimate(
            flops=logperm.size * 250, bytes_accessed=logperm.size * 16, transcendentals=logperm.size
        ),
        name="solve",
    )(logperm, source, observed)


def on_device(logperm, source, observed, brownian):
    particles, width, rows, depth = logperm.shape
    slabs, doms = lax.axis_size("slab"), lax.axis_size("dom")
    assert particles == slabs
    layers = width * slabs
    cells = layers * rows * depth
    ensemble = particles * doms
    whole = lax.all_to_all(logperm, "slab", split_axis=0, concat_axis=1, tiled=True)[0]
    full_source = lax.all_gather(source, "slab", axis=0, tiled=True)
    full_observed = lax.all_gather(observed, "slab", axis=0, tiled=True)
    u_cells = lax.all_to_all(
        logperm.reshape(particles, -1), "dom", split_axis=1, concat_axis=0, tiled=True
    )
    centre = jnp.mean(u_cells, axis=0, keepdims=True)
    spread = u_cells - centre
    gradient = solve(whole, full_source, full_observed)
    g_slab = lax.all_to_all(
        gradient.reshape(slabs, 1, -1), "slab", split_axis=0, concat_axis=1, tiled=True
    )[0]
    g_cells = lax.all_to_all(g_slab, "dom", split_axis=1, concat_axis=0, tiled=True)
    partial_gram = lax.dot_general(
        spread,
        g_cells,
        (((1,), (1,)), ((), ())),
        precision=lax.Precision.HIGHEST,
        preferred_element_type=jnp.float32,
    )
    gram = lax.psum(partial_gram, ("dom", "slab"))
    step_size = ensemble / (4.0 * (cells + 1))
    mixing = -(step_size / ensemble) * gram + math.sqrt(2.0 * step_size / ensemble) * brownian
    moved = (
        centre
        + 1.25 * spread
        + lax.dot_general(
            mixing,
            spread,
            (((0,), (0,)), ((), ())),
            precision=lax.Precision.HIGHEST,
            preferred_element_type=jnp.float32,
        )
    )
    returned = lax.all_to_all(moved, "dom", split_axis=0, concat_axis=1, tiled=True)
    return returned.reshape(logperm.shape)


def solution(mesh):
    return jax.shard_map(
        on_device,
        mesh=mesh,
        in_specs=(P("dom", "slab", None, None), P("slab", None, None), P("slab", None, None), P()),
        out_specs=P("dom", "slab", None, None),
        check_vma=False,
    )
```

time: 234 us -> 152 us (0.65)
  starting transfers between devices: 109 us -> 18 us
  Pallas kernels: 0 us -> 16.5 us
  blocking collectives: 59.9 us -> 76.2 us
  waiting for transfers between devices: 42.8 us -> 33.5 us
  other arithmetic: 10.5 us -> 2.49 us
  local copies, waits for them, and re-layouts: 8.39 us -> 3.13 us
    ppermute x32 -> x0, starting transfers between devices: 97.4 us -> none  [the longest x16 76.6 us: with_halo(): lax.ppermute(lax.slice_in_dim(block, block.shape[dim] - width, None, axis...]
    ppermute x32 -> x0, waiting for transfers between devices: 31.8 us -> none  [the longest x16 31.8 us: with_halo(): lax.ppermute(lax.slice_in_dim(block, 0, width, axis=dim), axis, backward)]
    all_gather x0 -> x2, blocking collectives: none -> 19.8 us  [the longest x1 12.5 us: on_device(): full_source = lax.all_gather(source, 'slab', axis=0, tiled=True)]
    pallas_call x0 -> x1, Pallas kernels: none -> 16.5 us  [solve(): pl.pallas_call(solve_kernel, out_shape=jax.ShapeDtypeStruct(logperm.shape...]
    all_to_all x1, waiting for transfers between devices: 0.01 us -> 12 us  [on_device(): lax.all_to_all(logperm.reshape(particles, -1), 'dom', split_axis=1, conca...]
    all_to_all x1 -> x3, waiting for transfers between devices: 11 us -> 21.5 us  [the longest x1 14 us: on_device(): lax.all_to_all(g_slab, 'dom', split_axis=1, concat_axis=0, tiled=True)]
    mul x15 -> x0, other arithmetic: 7.75 us -> none  [the longest x12 5.86 us: relax_rim(): inverse * (rhs + e_core * neighbor_sum(value, bordered[:, :-2], bordered[...]
    all_to_all x1 -> x3, starting transfers between devices: 6.02 us -> 11.6 us  [the longest x1 4.37 us: on_device(): lax.all_to_all(logperm, 'slab', split_axis=0, concat_axis=1, tiled=True)[0]]
  transfers between devices with their start and end apart: 34 -> 4, of which waited for: 16 -> 3; matrix products, arithmetic and copies ran while one was open for 2% -> 3% of each run, Pallas kernels for 0% -> 0%
where the time goes in v1:
time: 152 us; the launch traced here: 151 us
  blocking collectives  76.2 us (50%)
  waiting for transfers between devices  33.5 us (22%)
  starting transfers between devices  18 us (12%)
  Pallas kernels  16.5 us (11%)
  local copies, waits for them, and re-layouts  3.13 us (2%)
  other arithmetic  2.49 us (2%)
    psum x1, blocking collectives, on_device(): gram = lax.psum(partial_gram, ('dom', 'slab'))  38.6 us
    all_to_all x1, blocking collectives, on_device(): lax.all_to_all(moved, 'dom', split_axis=0, concat_axis=1, tiled=True)  17.8 us
    pallas_call x1, Pallas kernels, solve(): pl.pallas_call(solve_kernel, out_shape=jax.ShapeDtypeStruct(logperm.shape...  16.5 us
    all_to_all x1, waiting for transfers between devices, on_device(): lax.all_to_all(g_slab, 'dom', split_axis=1, concat_axis=0, tiled=True)  14 us
    all_gather x1, blocking collectives, on_device(): full_source = lax.all_gather(source, 'slab', axis=0, tiled=True)  12.5 us
    all_to_all x1, waiting for transfers between devices, on_device(): lax.all_to_all(logperm.reshape(particles, -1), 'dom', split_axis=1, conca...  12 us
    all_to_all x1, waiting for transfers between devices, on_device(): lax.all_to_all(gradient.reshape(slabs, 1, -1), 'slab', split_axis=0, conc...  7.56 us
    all_gather x1, blocking collectives, on_device(): full_observed = lax.all_gather(observed, 'slab', axis=0, tiled=True)  7.28 us
  transfers between devices with their start and end apart: 4, of which 3 were waited for; matrix products, arithmetic and copies ran while one was open for 3% of the time, Pallas kernels for 0%

profile of v1, /device:TPU:0, one launch (start us, length us, event | category | flops | bytes accessed | tf_op | source)
XLA Modules:
  0.0 151.2 jit_solution(14753771777018726670)
XLA Ops:
  0.0 0.0 copy-start.1
  0.0 4.4 %all-to-all-start.1 = ((f32[4,4,64,128]{3,2,1,0:T(8,128)}), f32[4,4,64,128]{3,2,1,0:T(8,128)S(1)}, u32[]{:S(2)}, u32[]{:S(2)}) async-start(f32[4,4,64,128]{3,2,1,0:T(8,128)} %param.4), calls=%async_computation.1 | async-start | bytes 1048576 | tf_op jit(solution)/shard_map/all_to_all | solution.py:174
  4.4 0.0 copy-done.1
  4.4 0.0 copy-start.2
  4.4 12.5 %all_gather.6.source = f32[16,64,128]{2,1,0:T(8,128)S(1)} all-gather(f32[4,64,128]{2,1,0:T(8,128)S(1)} %copy-done.1), channel_id=1, replica_groups=mesh['dom'=8,'slab'=4] {'slab'}, dimensions={0}, use_global_device_ids=true | all-gather | bytes 655360 | tf_op jit(solution)/shard_map/all_gather | solution.py:175
  16.9 0.0 copy-done.2
  16.9 7.3 %all_gather.7.observed = f32[16,64,128]{2,1,0:T(8,128)S(1)} all-gather(f32[4,64,128]{2,1,0:T(8,128)S(1)} %copy-done.2), channel_id=1, replica_groups=mesh['dom'=8,'slab'=4] {'slab'}, dimensions={0}, use_global_device_ids=true | all-gather | bytes 655360 | tf_op jit(solution)/shard_map/all_gather | solution.py:176
  24.2 0.0 all-to-all-done.1
  24.2 16.5 %solve.1 = f32[16,64,128]{2,1,0:T(8,128)} custom-call(f32[16,64,128]{2,1,0:T(8,128)S(1)} %bitcast.11, f32[16,64,128]{2,1,0:T(8,128)S(1)} %all_gather.6.source, f32[16,64,128]{2,1,0:T(8,128)S(1)} %all_gather.7.observed), custom_call_target="tpu_custom_call" | custom-call | flops 32768000 | bytes 2097152 | tf_op jit(solution)/shard_map/solve/pallas_call | solution.py:153
  40.7 0.0 copy-start
  40.7 3.6 %all-to-all-start.2 = ((f32[4,1,32768]{2,1,0:T(1,128)}), f32[4,1,32768]{2,1,0:T(1,128)S(1)}, u32[]{:S(2)}, u32[]{:S(2)}) async-start(f32[4,1,32768]{2,1,0:T(1,128)} %bitcast.2), calls=%async_computation.2 | async-start | bytes 1048576 | tf_op jit(solution)/shard_map/all_to_all | solution.py:183
  44.3 0.0 copy-done
  44.3 0.1 all_to_all.54
  44.4 1.1 copy.9
  45.6 7.6 %all-to-all-done.2 = f32[4,1,32768]{2,1,0:T(1,128)S(1)} async-done(((f32[4,1,32768]{2,1,0:T(1,128)}), f32[4,1,32768]{2,1,0:T(1,128)S(1)}, u32[]{:S(2)}, u32[]{:S(2)}) %all-to-all-start.2) | async-done | bytes 524320 | tf_op jit(solution)/shard_map/all_to_all | solution.py:183
  53.1 6.5 %all-to-all-start = ((f32[4,8,4096]{2,0,1:T(4,128)}), f32[4,8,4096]{2,0,1:T(4,128)S(1)}, u32[]{:S(2)}, u32[]{:S(2)}) async-start(f32[4,8,4096]{2,0,1:T(4,128)} %copy.9), calls=%async_computation | async-start | bytes 1048576 | tf_op jit(solution)/shard_map/all_to_all | solution.py:177
  59.6 2.3 %reduce.2 = f32[4,32768]{1,0:T(4,128)} reduce(f32[4,1,32768]{2,1,0:T(1,128)S(1)} %all-to-all-done.2, f32[]{:T(128)} %constant.12), dimensions={1}, to_apply=%all_to_all.59.reduce_sub_computation | reduce | bytes 1048580 | tf_op jit(solution)/shard_map/all_to_all | solution.py:183
  61.9 12.0 %all-to-all-done = f32[4,8,4096]{2,0,1:T(4,128)S(1)} async-done(((f32[4,8,4096]{2,0,1:T(4,128)}), f32[4,8,4096]{2,0,1:T(4,128)S(1)}, u32[]{:S(2)}, u32[]{:S(2)}) %all-to-all-start) | async-done | bytes 524320 | tf_op jit(solution)/shard_map/all_to_all | solution.py:177
  73.9 3.6 %all-to-all-start.3 = ((f32[4,8,4096]{2,0,1:T(4,128)}), f32[4,8,4096]{2,0,1:T(4,128)S(1)}, u32[]{:S(2)}, u32[]{:S(2)}) async-start(f32[4,8,4096]{2,0,1:T(4,128)} %bitcast.5), calls=%async_computation.3 | async-start | bytes 1048576 | tf_op jit(solution)/shard_map/all_to_all | solution.py:186
  77.5 0.1 reduce_sum.9
  77.6 0.1 broadcast_subtract_fusion
  77.7 0.2 sub.13
  77.9 0.2 all_to_all.57
  78.1 14.0 %all-to-all-done.3 = f32[4,8,4096]{2,0,1:T(4,128)S(1)} async-done(((f32[4,8,4096]{2,0,1:T(4,128)}), f32[4,8,4096]{2,0,1:T(4,128)S(1)}, u32[]{:S(2)}, u32[]{:S(2)}) %all-to-all-start.3) | async-done | bytes 524320 | tf_op jit(solution)/shard_map/all_to_all | solution.py:186
  92.1 0.2 all_to_all.63
  92.3 0.6 fusion.9
  92.8 0.0 copy-start.3
  92.8 38.6 %psum.7 = f32[32,32]{1,0:T(8,128)S(1)} all-reduce(f32[32,32]{1,0:T(8,128)S(1)} %fusion.9), channel_id=1, replica_groups=mesh['dom'=8,'slab'=4] {'dom','slab'}, use_global_device_ids=true, to_apply=%region_1.0 | all-reduce | flops 1024 | bytes 8192 | tf_op jit(solution)/shard_map/psum | solution.py:194
  131.4 0.0 copy-done.3
  131.4 0.6 convolution_add_fusion
  132.1 0.1 all_to_all.64
  132.2 17.8 %all_to_all.72 = f32[8,4,4096]{2,1,0:T(4,128)S(1)} all-to-all(f32[8,4,4096]{2,1,0:T(4,128)S(1)} %all_to_all.64), channel_id=1, replica_groups=mesh['dom'=8,'slab'=4] {'dom'}, dimensions={0} | all-to-all | bytes 1048576 | tf_op jit(solution)/shard_map/all_to_all | solution.py:208
  150.0 0.3 copy.12
  150.3 0.9 reshape.38
  (1 shorter events, 0.0 us)
Async XLA Ops:
  0.0 4.4 %copy-start.1 = (f32[4,64,128]{2,1,0:T(8,128)S(1)}, f32[4,64,128]{2,1,0:T(8,128)}, u32[]{:S(2)}) copy-start(f32[4,64,128]{2,1,0:T(8,128)} %param.5) | copy-start | bytes 393220
  0.0 24.2 %all-to-all-start.1 = ((f32[4,4,64,128]{3,2,1,0:T(8,128)}), f32[4,4,64,128]{3,2,1,0:T(8,128)S(1)}, u32[]{:S(2)}, u32[]{:S(2)}) async-start(f32[4,4,64,128]{3,2,1,0:T(8,128)} %param.4), calls=%async_computation.1 | async-start | bytes 1048576 | tf_op jit(solution)/shard_map/all_to_all | solution.py:174
  4.4 12.5 %copy-start.2 = (f32[4,64,128]{2,1,0:T(8,128)S(1)}, f32[4,64,128]{2,1,0:T(8,128)}, u32[]{:S(2)}) copy-start(f32[4,64,128]{2,1,0:T(8,128)} %param.6) | copy-start | bytes 393220
  40.7 3.6 %copy-start = (f32[4,4,64,128]{3,2,1,0:T(8,128)S(1)}, f32[4,4,64,128]{3,2,1,0:T(8,128)}, u32[]{:S(2)}) copy-start(f32[4,4,64,128]{3,2,1,0:T(8,128)} %param.4) | copy-start | bytes 1572868
  40.7 12.4 %all-to-all-start.2 = ((f32[4,1,32768]{2,1,0:T(1,128)}), f32[4,1,32768]{2,1,0:T(1,128)S(1)}, u32[]{:S(2)}, u32[]{:S(2)}) async-start(f32[4,1,32768]{2,1,0:T(1,128)} %bitcast.2), calls=%async_computation.2 | async-start | bytes 1048576 | tf_op jit(solution)/shard_map/all_to_all | solution.py:183
  53.1 20.8 %all-to-all-start = ((f32[4,8,4096]{2,0,1:T(4,128)}), f32[4,8,4096]{2,0,1:T(4,128)S(1)}, u32[]{:S(2)}, u32[]{:S(2)}) async-start(f32[4,8,4096]{2,0,1:T(4,128)} %copy.9), calls=%async_computation | async-start | bytes 1048576 | tf_op jit(solution)/shard_map/all_to_all | solution.py:177
  73.9 18.2 %all-to-all-start.3 = ((f32[4,8,4096]{2,0,1:T(4,128)}), f32[4,8,4096]{2,0,1:T(4,128)S(1)}, u32[]{:S(2)}, u32[]{:S(2)}) async-start(f32[4,8,4096]{2,0,1:T(4,128)} %bitcast.5), calls=%async_computation.3 | async-start | bytes 1048576 | tf_op jit(solution)/shard_map/all_to_all | solution.py:186
  92.8 38.6 %copy-start.3 = (f32[32,32]{1,0:T(8,128)S(1)}, f32[32,32]{1,0:T(8,128)}, u32[]{:S(2)}) copy-start(f32[32,32]{1,0:T(8,128)} %param.7) | copy-start | bytes 12292

commit v2 on v1

--- a/solution.py
+++ b/solution.py
@@ -129,84 +129,297 @@
     return -0.5 * e_core * total
 
 
-def solve_kernel(logperm, source, observed, gradient, *fields):
-    layers, rows, depth = gradient.shape
+def fused_kernel(
+    logperm, source, observed, brownian, moved_out,
+    whole, full_source, full_observed, gradient, members, spread, centre, owned, moved, parts,
+    noise, slab_send, slab_recv, side_send, side_recv, member_send, member_recv, own_sem,
+    gradient_send, gradient_recv, part_send, part_recv, result_send, result_recv, *fields,
+):
+    dom, slab = lax.axis_index("dom"), lax.axis_index("slab")
+    doms, slabs = lax.axis_size("dom"), lax.axis_size("slab")
+    particles, width, rows, depth = logperm.shape
+    layers = width * slabs
+    team = width
+    crew = team * slabs
+    ensemble = doms * particles
+    place = lax.rem(dom, team)
+    base = dom - place
+    mine = slab * width + place
+    column = place * particles + slab
+
+    def remote(src, dst, send, recv, at_dom, at_slab):
+        return pltpu.make_async_remote_copy(
+            src_ref=src, dst_ref=dst, send_sem=send, recv_sem=recv,
+            device_id=(at_dom, at_slab), device_id_type=pl.DeviceIdType.MESH,
+        )
+
+    def crew_device(step):
+        layer = lax.rem(mine + step, layers)
+        return layer, base + lax.rem(layer, width), layer // width
+
+    barrier = pltpu.get_barrier_semaphore()
+
+    def greet_dom(step, carry):
+        pl.semaphore_signal(
+            barrier, inc=1, device_id=(lax.rem(dom + step, doms), slab), device_id_type=pl.DeviceIdType.MESH
+        )
+        return carry
+
+    lax.fori_loop(1, doms, greet_dom, 0)
+
+    def greet_slab(step, carry):
+        near = lax.rem(slab + 1 + step // team, slabs)
+        pl.semaphore_signal(
+            barrier, inc=1, device_id=(base + lax.rem(step, team), near), device_id_type=pl.DeviceIdType.MESH
+        )
+        return carry
+
+    lax.fori_loop(0, crew - team, greet_slab, 0)
     set_borders(fields, layers, rows, depth)
-    coefficients(lambda layer: logperm[layer], fields)
-    relax(lambda layer: source[layer], fields[1], fields[2], fields)
+    noise[...] = brownian[...].T
+    pl.semaphore_wait(barrier, doms - 1 + crew - team)
+
+    own_block = pltpu.make_async_copy(logperm.at[slab], whole.at[pl.ds(slab * width, width)], own_sem.at[0])
+    own_block.start()
+
+    def slab_copy(step):
+        near = lax.rem(slab + step, slabs)
+        return remote(
+            logperm.at[near], whole.at[pl.ds(slab * width, width)],
+            slab_send.at[step - 1], slab_recv.at[step - 1], dom, near,
+        )
+
+    order = [2, 1, 3]
+    for step in order:
+        slab_copy(step).start()
+
+    across = lax.rem(slab + 2, slabs)
+    beside = slab + 1 - 2 * lax.rem(slab, 2)
+    local = []
+
+    def side_copies(which, block, full):
+        def at(owner):
+            return full.at[pl.ds(owner * width, width)]
+
+        return [
+            remote(block, at(slab), side_send.at[which, 0], side_recv.at[which, 0], dom, across),
+            remote(block, at(slab), side_send.at[which, 1], side_recv.at[which, 1], dom, beside),
+            remote(at(across), at(across), side_send.at[which, 2], side_recv.at[which, 2], dom, beside),
+        ]
+
+    sides = [side_copies(0, source, full_source), side_copies(1, observed, full_observed)]
+    for which, (block, full) in enumerate(((source, full_source), (observed, full_observed))):
+        copy = pltpu.make_async_copy(block, full.at[pl.ds(slab * width, width)], own_sem.at[1 + which])
+        copy.start()
+        local.append(copy)
+    sides[0][0].start()
+    sides[0][1].start()
+
+    def member_copy(step):
+        target = lax.rem(dom + step, doms)
+        return remote(
+            logperm.at[:, lax.rem(target, team)], members.at[pl.ds(dom * particles, particles)],
+            member_send.at[step - 1], member_recv.at[step - 1], target, slab,
+        )
+
+    def start_member(step, carry):
+        member_copy(step).start()
+        return carry
+
+    lax.fori_loop(1, doms, start_member, 0)
+    own_members = pltpu.make_async_copy(
+        logperm.at[:, place], members.at[pl.ds(dom * particles, particles)], own_sem.at[3]
+    )
+    own_members.start()
+    sides[1][0].start()
+    sides[1][1].start()
+
+    own_block.wait()
+    for step in order:
+        slab_copy(step).wait_recv()
+    coefficients(lambda layer: whole[layer], fields)
+    sides[0][0].wait_recv()
+    sides[0][2].start()
+    sides[0][1].wait_recv()
+    local[0].wait()
+    sides[0][2].wait_recv()
+    relax(lambda layer: full_source[layer], fields[1], fields[2], fields)
     pressure = fields[2]
+    sides[1][0].wait_recv()
+    sides[1][2].start()
+    sides[1][1].wait_recv()
+    local[1].wait()
+    sides[1][2].wait_recv()
 
     def misfit(layer):
-        return misfit_weight * (pressure[layer + 1, TOP : TOP + rows] - observed[layer])
+        return misfit_weight * (pressure[layer + 1, TOP : TOP + rows] - full_observed[layer])
 
     relax(misfit, fields[1], fields[3], fields)
 
-    def store(layer, carry):
+    def gradient_copy(step):
+        layer, at_dom, at_slab = crew_device(step)
+        return remote(
+            gradient.at[layer], owned.at[pl.ds(column * rows, rows)],
+            gradient_send.at[step - 1], gradient_recv.at[step - 1], at_dom, at_slab,
+        )
+
+    def send_gradient(step, carry):
+        layer = lax.rem(mine + step, layers)
         gradient[layer] = gradient_layer(layer, fields)
-        return carry
-
-    lax.fori_loop(0, layers, store, 0)
-
-
-def solve(logperm, source, observed):
-    layers, rows, depth = logperm.shape
-    return pl.pallas_call(
-        solve_kernel,
-        out_shape=jax.ShapeDtypeStruct(logperm.shape, jnp.float32),
-        in_specs=[pl.BlockSpec(memory_space=pltpu.VMEM)] * 3,
-        out_specs=pl.BlockSpec(memory_space=pltpu.VMEM),
-        scratch_shapes=scratch_fields(layers, rows, depth),
-        compiler_params=pltpu.CompilerParams(vmem_limit_bytes=VMEM_BYTES),
-        cost_estimate=pl.CostEstimate(
-            flops=logperm.size * 250, bytes_accessed=logperm.size * 16, transcendentals=logperm.size
-        ),
-        name="solve",
-    )(logperm, source, observed)
+        gradient_copy(step).start()
+        return carry
+
+    lax.fori_loop(1, layers, send_gradient, 0)
+    owned[pl.ds(column * rows, rows)] = gradient_layer(mine, fields)
+
+    def wait_member(step, carry):
+        member_copy(step).wait_recv()
+        return carry
+
+    own_members.wait()
+    lax.fori_loop(1, doms, wait_member, 0)
+    for row in range(rows):
+        across_cells = members[:, row]
+        mean = jnp.sum(across_cells, axis=0, keepdims=True) * (1.0 / ensemble)
+        spread[:, row * depth : (row + 1) * depth] = across_cells - mean
+        centre[:, row * depth : (row + 1) * depth] = mean
+
+    def wait_gradient(step, carry):
+        gradient_copy(step).wait_recv()
+        return carry
+
+    lax.fori_loop(1, crew, wait_gradient, 0)
+    gram = jnp.zeros((crew, ensemble), jnp.float32)
+    piece = min(16, rows)
+    for first in range(0, rows, piece):
+        held = [owned[pl.ds(row, crew, stride=rows)] for row in range(first, first + piece)]
+        gram = gram + lax.dot_general(
+            jnp.concatenate(held, axis=1),
+            spread[:, first * depth : (first + piece) * depth],
+            (((1,), (1,)), ((), ())),
+            precision=lax.Precision.HIGHEST,
+            preferred_element_type=jnp.float32,
+        )
+    parts[mine] = gram
+
+    def part_copy(step):
+        _, at_dom, at_slab = crew_device(step)
+        return remote(
+            parts.at[mine], parts.at[mine], part_send.at[step - 1], part_recv.at[step - 1], at_dom, at_slab
+        )
+
+    def start_part(step, carry):
+        part_copy(step).start()
+        return carry
+
+    def wait_part(step, carry):
+        part_copy(step).wait_recv()
+        return carry
+
+    lax.fori_loop(1, crew, start_part, 0)
+    lax.fori_loop(1, crew, wait_part, 0)
+    gram = jnp.sum(parts[...], axis=0)
+    step_size = ensemble / (4.0 * (layers * rows * depth + 1))
+    first_column = pl.multiple_of(base * particles, 8)
+    mixing = -(step_size / ensemble) * gram + math.sqrt(2.0 * step_size / ensemble) * noise[
+        pl.ds(first_column, crew)
+    ]
+    for first in range(0, rows, piece):
+        cells = slice(first * depth, (first + piece) * depth)
+        result = (
+            centre[:, cells]
+            + 1.25 * spread[pl.ds(first_column, crew), cells]
+            + lax.dot_general(
+                mixing, spread[:, cells], (((1,), (0,)), ((), ())),
+                precision=lax.Precision.HIGHEST, preferred_element_type=jnp.float32,
+            )
+        )
+        for row in range(piece):
+            moved[pl.ds(first + row, crew, stride=rows)] = result[:, row * depth : (row + 1) * depth]
+
+    def result_copy(step):
+        to = lax.rem(place + step, team)
+        return remote(
+            moved_rows(to), moved_out.at[:, pl.ds(place * rows, rows)],
+            result_send.at[step - 1], result_recv.at[step - 1], base + to, slab,
+        )
+
+    def moved_rows(to):
+        return moved.reshape(crew, rows, depth).at[pl.ds(to * particles, particles)]
+
+    for step in range(1, team):
+        result_copy(step).start()
+    own_result = pltpu.make_async_copy(
+        moved_rows(place), moved_out.at[:, pl.ds(place * rows, rows)], own_sem.at[4]
+    )
+    own_result.start()
+
+    for step in order:
+        slab_copy(step).wait_send()
+    for which in range(2):
+        for copy in sides[which]:
+            copy.wait_send()
+
+    def sent_member(step, carry):
+        member_copy(step).wait_send()
+        return carry
+
+    def sent_crew(step, carry):
+        gradient_copy(step).wait_send()
+        part_copy(step).wait_send()
+        return carry
+
+    lax.fori_loop(1, doms, sent_member, 0)
+    lax.fori_loop(1, crew, sent_crew, 0)
+    own_result.wait()
+    for step in range(1, team):
+        result_copy(step).wait()
 
 
 def on_device(logperm, source, observed, brownian):
     particles, width, rows, depth = logperm.shape
     slabs, doms = lax.axis_size("slab"), lax.axis_size("dom")
-    assert particles == slabs
-    layers = width * slabs
-    cells = layers * rows * depth
-    ensemble = particles * doms
-    whole = lax.all_to_all(logperm, "slab", split_axis=0, concat_axis=1, tiled=True)[0]
-    full_source = lax.all_gather(source, "slab", axis=0, tiled=True)
-    full_observed = lax.all_gather(observed, "slab", axis=0, tiled=True)
-    u_cells = lax.all_to_all(
-        logperm.reshape(particles, -1), "dom", split_axis=1, concat_axis=0, tiled=True
-    )
-    centre = jnp.mean(u_cells, axis=0, keepdims=True)
-    spread = u_cells - centre
-    gradient = solve(whole, full_source, full_observed)
-    g_slab = lax.all_to_all(
-        gradient.reshape(slabs, 1, -1), "slab", split_axis=0, concat_axis=1, tiled=True
-    )[0]
-    g_cells = lax.all_to_all(g_slab, "dom", split_axis=1, concat_axis=0, tiled=True)
-    partial_gram = lax.dot_general(
-        spread,
-        g_cells,
-        (((1,), (1,)), ((), ())),
-        precision=lax.Precision.HIGHEST,
-        preferred_element_type=jnp.float32,
-    )
-    gram = lax.psum(partial_gram, ("dom", "slab"))
-    step_size = ensemble / (4.0 * (cells + 1))
-    mixing = -(step_size / ensemble) * gram + math.sqrt(2.0 * step_size / ensemble) * brownian
-    moved = (
-        centre
-        + 1.25 * spread
-        + lax.dot_general(
-            mixing,
-            spread,
-            (((0,), (0,)), ((), ())),
-            precision=lax.Precision.HIGHEST,
-            preferred_element_type=jnp.float32,
-        )
-    )
-    returned = lax.all_to_all(moved, "dom", split_axis=0, concat_axis=1, tiled=True)
-    return returned.reshape(logperm.shape)
+    assert particles == slabs == 4 and doms % width == 0
+    layers, crew, ensemble = width * slabs, width * slabs, doms * particles
+    f32 = jnp.float32
+    dma = pltpu.SemaphoreType.DMA
+    scratch = [
+        pltpu.VMEM((layers, rows, depth), f32),
+        pltpu.VMEM((layers, rows, depth), f32),
+        pltpu.VMEM((layers, rows, depth), f32),
+        pltpu.VMEM((layers, rows, depth), f32),
+        pltpu.VMEM((ensemble, rows, depth), f32),
+        pltpu.VMEM((ensemble, rows * depth), f32),
+        pltpu.VMEM((1, rows * depth), f32),
+        pltpu.VMEM((crew * rows, depth), f32),
+        pltpu.VMEM((crew * rows, depth), f32),
+        pltpu.VMEM((crew, crew, ensemble), f32),
+        pltpu.VMEM((ensemble, ensemble), f32),
+        dma((slabs - 1,)), dma((slabs - 1,)),
+        dma((2, 3)), dma((2, 3)),
+        dma((doms - 1,)), dma((doms - 1,)),
+        dma((5,)),
+        dma((crew - 1,)), dma((crew - 1,)),
+        dma((crew - 1,)), dma((crew - 1,)),
+        dma((width - 1,)), dma((width - 1,)),
+        *scratch_fields(layers, rows, depth),
+    ]
+    anywhere = pl.BlockSpec(memory_space=pl.ANY)
+    moved = pl.pallas_call(
+        fused_kernel,
+        out_shape=jax.ShapeDtypeStruct((particles, width * rows, depth), f32),
+        in_specs=[anywhere] * 3 + [pl.BlockSpec(memory_space=pltpu.VMEM)],
+        out_specs=anywhere,
+        scratch_shapes=scratch,
+        compiler_params=pltpu.CompilerParams(
+            collective_id=0, has_side_effects=True, vmem_limit_bytes=VMEM_BYTES
+        ),
+        cost_estimate=pl.CostEstimate(
+            flops=logperm.size * 300, bytes_accessed=logperm.size * 16, transcendentals=logperm.size
+        ),
+        name="langevin",
+    )(logperm, source, observed, brownian)
+    return moved.reshape(logperm.shape)
 
 
 def solution(mesh):

time: 152 us -> 58.6 us (0.39)
  blocking collectives: 76.2 us -> 0 us
  Pallas kernels: 16.5 us -> 54 us
  waiting for transfers between devices: 33.5 us -> 0 us
  starting transfers between devices: 18 us -> 0 us
  other arithmetic: 2.49 us -> 0 us
    psum x1 -> x0, blocking collectives: 38.6 us -> none  [on_device(): gram = lax.psum(partial_gram, ('dom', 'slab'))]
    pallas_call x1, Pallas kernels: 16.5 us -> 54 us  [on_device(): pl.pallas_call(fused_kernel, out_shape=jax.ShapeDtypeStruct((particles, w...]
    all_to_all x4 -> x0, waiting for transfers between devices: 33.5 us -> none  [the longest x1 14 us: on_device(): lax.all_to_all(g_slab, 'dom', split_axis=1, concat_axis=0, tiled=True)]
    all_gather x2 -> x0, blocking collectives: 19.8 us -> none  [the longest x1 12.5 us: on_device(): full_source = lax.all_gather(source, 'slab', axis=0, tiled=True)]
    all_to_all x4 -> x0, starting transfers between devices: 18 us -> none  [the longest x1 6.46 us: on_device(): lax.all_to_all(logperm.reshape(particles, -1), 'dom', split_axis=1, conca...]
    all_to_all x1 -> x0, blocking collectives: 17.8 us -> none  [on_device(): lax.all_to_all(moved, 'dom', split_axis=0, concat_axis=1, tiled=True)]
    unnamed x8 -> x9, local copies, waits for them, and re-layouts: 0.02 us -> 4.36 us
    all_to_all x1 -> x0, other arithmetic: 2.28 us -> none  [on_device(): lax.all_to_all(gradient.reshape(slabs, 1, -1), 'slab', split_axis=0, conc...]
  transfers between devices with their start and end apart: 4 -> 0, of which waited for: 3 -> 0; matrix products, arithmetic and copies ran while one was open for 3% -> 0% of each run, Pallas kernels for 0% -> 0%
where the time goes in v2:
time: 58.6 us; the launch traced here: 58.3 us
  Pallas kernels  54 us (92%)
  local copies, waits for them, and re-layouts  4.36 us (7%)
    pallas_call x1, Pallas kernels, on_device(): pl.pallas_call(fused_kernel, out_shape=jax.ShapeDtypeStruct((particles, w...  54 us
    unnamed x9, local copies, waits for them, and re-layouts  4.36 us

profile of v2, /device:TPU:0, one launch (start us, length us, event | category | flops | bytes accessed | tf_op | source)
XLA Modules:
  0.0 58.3 jit_solution(8553025121925700961)
XLA Ops:
  0.0 0.0 copy-start
  0.0 1.0 %copy-done = f32[4,4,64,128]{3,2,1,0:T(8,128)S(1)} copy-done((f32[4,4,64,128]{3,2,1,0:T(8,128)S(1)}, f32[4,4,64,128]{3,2,1,0:T(8,128)}, u32[]{:S(2)}) %copy-start) | copy-done | bytes 524312
  1.0 0.0 copy-start.1
  1.0 0.9 %copy-done.1 = f32[4,64,128]{2,1,0:T(8,128)S(1)} copy-done((f32[4,64,128]{2,1,0:T(8,128)S(1)}, f32[4,64,128]{2,1,0:T(8,128)}, u32[]{:S(2)}) %copy-start.1) | copy-done | bytes 131096
  1.9 0.0 copy-start.2
  1.9 0.9 %copy-done.2 = f32[4,64,128]{2,1,0:T(8,128)S(1)} copy-done((f32[4,64,128]{2,1,0:T(8,128)S(1)}, f32[4,64,128]{2,1,0:T(8,128)}, u32[]{:S(2)}) %copy-start.2) | copy-done | bytes 131096
  2.9 0.0 copy-start.3
  2.9 0.7 %copy-done.3 = f32[32,32]{1,0:T(8,128)S(1)} copy-done((f32[32,32]{1,0:T(8,128)S(1)}, f32[32,32]{1,0:T(8,128)}, u32[]{:S(2)}) %copy-start.3) | copy-done | bytes 4120
  3.6 54.0 %langevin.1 = f32[4,256,128]{2,1,0:T(8,128)S(1)} custom-call(f32[4,4,64,128]{3,2,1,0:T(8,128)S(1)} %copy-done, f32[4,64,128]{2,1,0:T(8,128)S(1)} %copy-done.1, f32[4,64,128]{2,1,0:T(8,128)S(1)} %copy-done.2, f32[32,32]{1,0:T(8,128)S(1)} %copy-done.3), custom_call_target="tpu_custom_call" | custom-call | flops 39321600 | bytes 2097152 | tf_op jit(solution)/shard_map/langevin/pallas_call | solution.py:408
  57.5 0.8 %copy.6 = f32[4,4,64,128]{3,2,1,0:T(8,128)} copy(f32[4,4,64,128]{3,2,1,0:T(8,128)S(1)} %bitcast.1) | data formatting | bytes 1048576
Async XLA Ops:
  0.0 1.0 %copy-start = (f32[4,4,64,128]{3,2,1,0:T(8,128)S(1)}, f32[4,4,64,128]{3,2,1,0:T(8,128)}, u32[]{:S(2)}) copy-start(f32[4,4,64,128]{3,2,1,0:T(8,128)} %logperm.1) | copy-start | bytes 1572868
  1.0 0.9 %copy-start.1 = (f32[4,64,128]{2,1,0:T(8,128)S(1)}, f32[4,64,128]{2,1,0:T(8,128)}, u32[]{:S(2)}) copy-start(f32[4,64,128]{2,1,0:T(8,128)} %source.1) | copy-start | bytes 393220
  1.9 0.9 %copy-start.2 = (f32[4,64,128]{2,1,0:T(8,128)S(1)}, f32[4,64,128]{2,1,0:T(8,128)}, u32[]{:S(2)}) copy-start(f32[4,64,128]{2,1,0:T(8,128)} %observed.1) | copy-start | bytes 393220
  2.9 0.7 %copy-start.3 = (f32[32,32]{1,0:T(8,128)S(1)}, f32[32,32]{1,0:T(8,128)}, u32[]{:S(2)}) copy-start(f32[32,32]{1,0:T(8,128)} %brownian.1) | copy-start | bytes 12292

commit v3 on v2

--- a/solution.py
+++ b/solution.py
@@ -9,7 +9,7 @@
 
 SWEEPS = 8
 misfit_weight = 1000.0
-VMEM_BYTES = 48 * 1024 * 1024
+VMEM_BYTES = 64 * 1024 * 1024 - 128 * 1024
 TOP = 8
 
 
@@ -65,7 +65,7 @@
         e[layer + 1, TOP : TOP + rows] = jnp.exp(0.5 * logperm(layer))
         return carry
 
-    lax.fori_loop(0, layers, exponent, 0)
+    lax.fori_loop(0, layers, exponent, 0, unroll=8)
 
     def divide(layer, carry):
         core, near = neighbors(e, layer, rows, masks, 1.0)
@@ -74,7 +74,7 @@
         gain[layer] = core * total
         return carry
 
-    lax.fori_loop(0, layers, divide, 0)
+    lax.fori_loop(0, layers, divide, 0, unroll=8)
 
 
 def relax(rhs, ping, pong, fields):
@@ -88,7 +88,7 @@
         ping[layer + 1, TOP : TOP + rows] = value
         return carry
 
-    lax.fori_loop(0, layers, first, 0)
+    lax.fori_loop(0, layers, first, 0, unroll=8)
 
     def swept(old, layer):
         _, near = neighbors(old, layer, rows, masks, 0.0)
@@ -100,7 +100,7 @@
             new[layer + 1, TOP : TOP + rows] = swept(old, layer)
             return carry
 
-        lax.fori_loop(0, layers, one, 0, unroll=2)
+        lax.fori_loop(0, layers, one, 0, unroll=layers)
 
     def pair(index, carry):
         sweep(ping, pong)
@@ -113,7 +113,7 @@
         pong[layer + 1, TOP : TOP + rows] = swept(ping, layer) / e[layer + 1, TOP : TOP + rows]
         return carry
 
-    lax.fori_loop(0, layers, last, 0, unroll=2)
+    lax.fori_loop(0, layers, last, 0, unroll=layers)
 
 
 def gradient_layer(layer, fields):
@@ -130,8 +130,8 @@
 
 
 def fused_kernel(
-    logperm, source, observed, brownian, moved_out,
-    whole, full_source, full_observed, gradient, members, spread, centre, owned, moved, parts,
+    logperm, source, observed, brownian_far, moved_out,
+    brownian, whole, full_source, full_observed, gradient, members, spread, centre, owned, moved, parts,
     noise, slab_send, slab_recv, side_send, side_recv, member_send, member_recv, own_sem,
     gradient_send, gradient_recv, part_send, part_recv, result_send, result_recv, *fields,
 ):
@@ -157,6 +157,8 @@
         layer = lax.rem(mine + step, layers)
         return layer, base + lax.rem(layer, width), layer // width
 
+    fetch = pltpu.make_async_copy(brownian_far, brownian, own_sem.at[5])
+    fetch.start()
     barrier = pltpu.get_barrier_semaphore()
 
     def greet_dom(step, carry):
@@ -176,7 +178,6 @@
 
     lax.fori_loop(0, crew - team, greet_slab, 0)
     set_borders(fields, layers, rows, depth)
-    noise[...] = brownian[...].T
     pl.semaphore_wait(barrier, doms - 1 + crew - team)
 
     own_block = pltpu.make_async_copy(logperm.at[slab], whole.at[pl.ds(slab * width, width)], own_sem.at[0])
@@ -231,12 +232,14 @@
         logperm.at[:, place], members.at[pl.ds(dom * particles, particles)], own_sem.at[3]
     )
     own_members.start()
-    sides[1][0].start()
-    sides[1][1].start()
-
+
+    fetch.wait()
+    noise[...] = brownian[...].T
     own_block.wait()
     for step in order:
         slab_copy(step).wait_recv()
+    sides[1][0].start()
+    sides[1][1].start()
     coefficients(lambda layer: whole[layer], fields)
     sides[0][0].wait_recv()
     sides[0][2].start()
@@ -269,7 +272,7 @@
         gradient_copy(step).start()
         return carry
 
-    lax.fori_loop(1, layers, send_gradient, 0)
+    lax.fori_loop(1, layers, send_gradient, 0, unroll=3)
     owned[pl.ds(column * rows, rows)] = gradient_layer(mine, fields)
 
     def wait_member(step, carry):
@@ -278,8 +281,9 @@
 
     own_members.wait()
     lax.fori_loop(1, doms, wait_member, 0)
+    member_rows = members.reshape(ensemble * rows, depth)
     for row in range(rows):
-        across_cells = members[:, row]
+        across_cells = member_rows[pl.ds(row, ensemble, stride=rows)]
         mean = jnp.sum(across_cells, axis=0, keepdims=True) * (1.0 / ensemble)
         spread[:, row * depth : (row + 1) * depth] = across_cells - mean
         centre[:, row * depth : (row + 1) * depth] = mean
@@ -384,6 +388,7 @@
     f32 = jnp.float32
     dma = pltpu.SemaphoreType.DMA
     scratch = [
+        pltpu.VMEM((ensemble, ensemble), f32),
         pltpu.VMEM((layers, rows, depth), f32),
         pltpu.VMEM((layers, rows, depth), f32),
         pltpu.VMEM((layers, rows, depth), f32),
@@ -398,18 +403,18 @@
         dma((slabs - 1,)), dma((slabs - 1,)),
         dma((2, 3)), dma((2, 3)),
         dma((doms - 1,)), dma((doms - 1,)),
-        dma((5,)),
+        dma((6,)),
         dma((crew - 1,)), dma((crew - 1,)),
         dma((crew - 1,)), dma((crew - 1,)),
         dma((width - 1,)), dma((width - 1,)),
         *scratch_fields(layers, rows, depth),
     ]
-    anywhere = pl.BlockSpec(memory_space=pl.ANY)
+    far = pl.BlockSpec(memory_space=pltpu.HBM)
     moved = pl.pallas_call(
         fused_kernel,
         out_shape=jax.ShapeDtypeStruct((particles, width * rows, depth), f32),
-        in_specs=[anywhere] * 3 + [pl.BlockSpec(memory_space=pltpu.VMEM)],
-        out_specs=anywhere,
+        in_specs=[far] * 4,
+        out_specs=far,
         scratch_shapes=scratch,
         compiler_params=pltpu.CompilerParams(
             collective_id=0, has_side_effects=True, vmem_limit_bytes=VMEM_BYTES

time: 58.6 us -> 50.8 us (0.87)
  the two profiles are of different devices: /device:TPU:0 before, /device:TPU:17 now
where the time goes in v3:
time: 50.8 us; the launch traced here: 50.7 us
  Pallas kernels  48.8 us (96%)
  local copies, waits for them, and re-layouts  1.89 us (4%)
    pallas_call x1, Pallas kernels, on_device(): pl.pallas_call(fused_kernel, out_shape=jax.ShapeDtypeStruct((particles, w...  48.8 us
    unnamed x1, local copies, waits for them, and re-layouts  1.89 us

profile of v3, /device:TPU:17, one launch (start us, length us, event | category | flops | bytes accessed | tf_op | source)
XLA Modules:
  0.0 50.7 jit_solution(1318969257492582469)
XLA Ops:
  0.0 48.8 %langevin.1 = f32[4,256,128]{2,1,0:T(8,128)} custom-call(f32[4,4,64,128]{3,2,1,0:T(8,128)} %logperm.1, f32[4,64,128]{2,1,0:T(8,128)} %source.1, f32[4,64,128]{2,1,0:T(8,128)} %observed.1, f32[32,32]{1,0:T(8,128)} %brownian_far.1), custom_call_target="tpu_custom_call" | custom-call | flops 39321600 | bytes 2097152 | tf_op jit(solution)/shard_map/langevin/pallas_call | solution.py:413
  48.8 1.9 %copy.6 = f32[4,4,64,128]{3,2,1,0:T(8,128)} copy(f32[4,4,64,128]{3,2,1,0:T(8,128)} %bitcast.1) | data formatting | bytes 1048576

commit v4 on v3

--- a/solution.py
+++ b/solution.py
@@ -10,42 +10,40 @@
 SWEEPS = 8
 misfit_weight = 1000.0
 VMEM_BYTES = 64 * 1024 * 1024 - 128 * 1024
-TOP = 8
-
-
-def lane_masks(shape):
-    lane = lax.broadcasted_iota(jnp.int32, shape, len(shape) - 1)
-    return lane == 0, lane == shape[-1] - 1
-
-
-def along_lanes(value, masks, fill):
-    depth = value.shape[-1]
-    before = jnp.where(masks[0], fill, pltpu.roll(value, 1, value.ndim - 1))
-    after = jnp.where(masks[1], fill, pltpu.roll(value, depth - 1, value.ndim - 1))
-    return before, after
-
-
-def neighbors(ref, layer, rows, masks, fill):
-    core = ref[layer + 1, TOP : TOP + rows]
-    return core, (
-        ref[layer, TOP : TOP + rows],
-        ref[layer + 2, TOP : TOP + rows],
-        ref[layer + 1, TOP - 1 : TOP + rows - 1],
-        ref[layer + 1, TOP + 1 : TOP + rows + 1],
-        *along_lanes(core, masks, fill),
-    )
+SUB = 8
+
+
+def interleaved(ref, layer, rows):
+    step = rows // SUB
+    first = layer * rows
+    return jnp.concatenate([ref[pl.ds(first + v, SUB, stride=step)] for v in range(step)], axis=0)
+
+
+def edge_masks(depth):
+    lane = lax.broadcasted_iota(jnp.int32, (SUB, depth), 1)
+    sublane = lax.broadcasted_iota(jnp.int32, (SUB, depth), 0)
+    return lane == 0, lane == depth - 1, sublane == 0, sublane == SUB - 1
+
+
+def neighbors(ref, layer, masks, fill):
+    core = ref[layer + 1]
+    rows, depth = core.shape
+    tiles = [core[at : at + SUB] for at in range(0, rows, SUB)]
+    before = [jnp.where(masks[2], fill, pltpu.roll(tiles[-1], 1, 0))] + tiles[:-1]
+    after = tiles[1:] + [jnp.where(masks[3], fill, pltpu.roll(tiles[0], SUB - 1, 0))]
+    left = [jnp.where(masks[0], fill, pltpu.roll(tile, 1, 1)) for tile in tiles]
+    right = [jnp.where(masks[1], fill, pltpu.roll(tile, depth - 1, 1)) for tile in tiles]
+    joined = [jnp.concatenate(side, axis=0) for side in (before, after, left, right)]
+    return core, (ref[layer], ref[layer + 2], *joined)
 
 
 def border(ref, layers, rows, depth, fill):
-    ref[0] = jnp.full((rows + 2 * TOP, depth), fill, jnp.float32)
-    ref[layers + 1] = jnp.full((rows + 2 * TOP, depth), fill, jnp.float32)
-    edge = jnp.full((layers + 2, TOP, depth), fill, jnp.float32)
-    ref[:, 0:TOP] = edge
-    ref[:, TOP + rows :] = edge
+    ref[0] = jnp.full((rows, depth), fill, jnp.float32)
+    ref[layers + 1] = jnp.full((rows, depth), fill, jnp.float32)
 
 
 def scratch_fields(layers, rows, depth):
-    padded = pltpu.VMEM((layers + 2, rows + 2 * TOP, depth), jnp.float32)
+    padded = pltpu.VMEM((layers + 2, rows, depth), jnp.float32)
     plain = pltpu.VMEM((layers, rows, depth), jnp.float32)
     return [padded] * 4 + [plain] * 3
 
@@ -59,16 +57,16 @@
 def coefficients(logperm, fields):
     e, inverse, gain = fields[0], fields[4], fields[5]
     layers, rows, depth = inverse.shape
-    masks = lane_masks((rows, depth))
+    masks = edge_masks(depth)
 
     def exponent(layer, carry):
-        e[layer + 1, TOP : TOP + rows] = jnp.exp(0.5 * logperm(layer))
+        e[layer + 1] = jnp.exp(0.5 * logperm(layer))
         return carry
 
     lax.fori_loop(0, layers, exponent, 0, unroll=8)
 
     def divide(layer, carry):
-        core, near = neighbors(e, layer, rows, masks, 1.0)
+        core, near = neighbors(e, layer, masks, 1.0)
         total = 1.0 / (near[0] + near[1] + near[2] + near[3] + near[4] + near[5])
         inverse[layer] = total
         gain[layer] = core * total
@@ -80,24 +78,24 @@
 def relax(rhs, ping, pong, fields):
     e, inverse, gain, start = fields[0], fields[4], fields[5], fields[6]
     layers, rows, depth = inverse.shape
-    masks = lane_masks((rows, depth))
+    masks = edge_masks(depth)
 
     def first(layer, carry):
         value = inverse[layer] * rhs(layer)
         start[layer] = value
-        ping[layer + 1, TOP : TOP + rows] = value
+        ping[layer + 1] = value
         return carry
 
     lax.fori_loop(0, layers, first, 0, unroll=8)
 
     def swept(old, layer):
-        _, near = neighbors(old, layer, rows, masks, 0.0)
+        _, near = neighbors(old, layer, masks, 0.0)
         total = (near[0] + near[1]) + (near[2] + near[3]) + (near[4] + near[5])
         return start[layer] + gain[layer] * total
 
     def sweep(old, new):
         def one(layer, carry):
-            new[layer + 1, TOP : TOP + rows] = swept(old, layer)
+            new[layer + 1] = swept(old, layer)
             return carry
 
         lax.fori_loop(0, layers, one, 0, unroll=layers)
@@ -110,7 +108,7 @@
     lax.fori_loop(0, (SWEEPS - 2) // 2, pair, 0)
 
     def last(layer, carry):
-        pong[layer + 1, TOP : TOP + rows] = swept(ping, layer) / e[layer + 1, TOP : TOP + rows]
+        pong[layer + 1] = swept(ping, layer) / e[layer + 1]
         return carry
 
     lax.fori_loop(0, layers, last, 0, unroll=layers)
@@ -119,10 +117,10 @@
 def gradient_layer(layer, fields):
     e, pressure, adjoint = fields[0], fields[2], fields[3]
     _, rows, depth = fields[4].shape
-    masks = lane_masks((rows, depth))
-    e_core, e_near = neighbors(e, layer, rows, masks, 1.0)
-    p_core, p_near = neighbors(pressure, layer, rows, masks, 0.0)
-    q_core, q_near = neighbors(adjoint, layer, rows, masks, 0.0)
+    masks = edge_masks(depth)
+    e_core, e_near = neighbors(e, layer, masks, 1.0)
+    p_core, p_near = neighbors(pressure, layer, masks, 0.0)
+    q_core, q_near = neighbors(adjoint, layer, masks, 0.0)
     total = e_near[0] * (p_core - p_near[0]) * (q_core - q_near[0])
     for side in range(1, 6):
         total = total + e_near[side] * (p_core - p_near[side]) * (q_core - q_near[side])
@@ -180,13 +178,14 @@
     set_borders(fields, layers, rows, depth)
     pl.semaphore_wait(barrier, doms - 1 + crew - team)
 
-    own_block = pltpu.make_async_copy(logperm.at[slab], whole.at[pl.ds(slab * width, width)], own_sem.at[0])
+    whole_blocks = whole.reshape(layers, rows, depth)
+    own_block = pltpu.make_async_copy(logperm.at[slab], whole_blocks.at[pl.ds(slab * width, width)], own_sem.at[0])
     own_block.start()
 
     def slab_copy(step):
         near = lax.rem(slab + step, slabs)
         return remote(
-            logperm.at[near], whole.at[pl.ds(slab * width, width)],
+            logperm.at[near], whole_blocks.at[pl.ds(slab * width, width)],
             slab_send.at[step - 1], slab_recv.at[step - 1], dom, near,
         )
 
@@ -200,7 +199,7 @@
 
     def side_copies(which, block, full):
         def at(owner):
-            return full.at[pl.ds(owner * width, width)]
+            return full.reshape(layers, rows, depth).at[pl.ds(owner * width, width)]
 
         return [
             remote(block, at(slab), side_send.at[which, 0], side_recv.at[which, 0], dom, across),
@@ -210,24 +209,28 @@
 
     sides = [side_copies(0, source, full_source), side_copies(1, observed, full_observed)]
     for which, (block, full) in enumerate(((source, full_source), (observed, full_observed))):
-        copy = pltpu.make_async_copy(block, full.at[pl.ds(slab * width, width)], own_sem.at[1 + which])
+        copy = pltpu.make_async_copy(block, full.reshape(layers, rows, depth).at[pl.ds(slab * width, width)], own_sem.at[1 + which])
         copy.start()
         local.append(copy)
     sides[0][0].start()
     sides[0][1].start()
 
     def member_copy(step):
-        target = lax.rem(dom + step, doms)
+        target = lax.rem(base + team * (1 + step // team), doms) + lax.rem(place + step, team)
         return remote(
             logperm.at[:, lax.rem(target, team)], members.at[pl.ds(dom * particles, particles)],
-            member_send.at[step - 1], member_recv.at[step - 1], target, slab,
-        )
-
-    def start_member(step, carry):
-        member_copy(step).start()
-        return carry
-
-    lax.fori_loop(1, doms, start_member, 0)
+            member_send.at[step], member_recv.at[step], target, slab,
+        )
+
+    def each_member(act):
+        def body(step, carry):
+            act(member_copy(step))
+            return carry
+
+        lax.fori_loop(0, doms - team, body, 0)
+        lax.fori_loop(doms - team + 1, doms, body, 0)
+
+    each_member(lambda copy: copy.start())
     own_members = pltpu.make_async_copy(
         logperm.at[:, place], members.at[pl.ds(dom * particles, particles)], own_sem.at[3]
     )
@@ -240,13 +243,13 @@
         slab_copy(step).wait_recv()
     sides[1][0].start()
     sides[1][1].start()
-    coefficients(lambda layer: whole[layer], fields)
+    coefficients(lambda layer: interleaved(whole, layer, rows), fields)
     sides[0][0].wait_recv()
     sides[0][2].start()
     sides[0][1].wait_recv()
     local[0].wait()
     sides[0][2].wait_recv()
-    relax(lambda layer: full_source[layer], fields[1], fields[2], fields)
+    relax(lambda layer: interleaved(full_source, layer, rows), fields[1], fields[2], fields)
     pressure = fields[2]
     sides[1][0].wait_recv()
     sides[1][2].start()
@@ -255,7 +258,7 @@
     sides[1][2].wait_recv()
 
     def misfit(layer):
-        return misfit_weight * (pressure[layer + 1, TOP : TOP + rows] - full_observed[layer])
+        return misfit_weight * (pressure[layer + 1] - interleaved(full_observed, layer, rows))
 
     relax(misfit, fields[1], fields[3], fields)
 
@@ -272,15 +275,11 @@
         gradient_copy(step).start()
         return carry
 
-    lax.fori_loop(1, layers, send_gradient, 0, unroll=3)
+    lax.fori_loop(1, layers, send_gradient, 0, unroll=5)
     owned[pl.ds(column * rows, rows)] = gradient_layer(mine, fields)
 
-    def wait_member(step, carry):
-        member_copy(step).wait_recv()
-        return carry
-
     own_members.wait()
-    lax.fori_loop(1, doms, wait_member, 0)
+    each_member(lambda copy: copy.wait_recv())
     member_rows = members.reshape(ensemble * rows, depth)
     for row in range(rows):
         across_cells = member_rows[pl.ds(row, ensemble, stride=rows)]
@@ -295,8 +294,12 @@
     lax.fori_loop(1, crew, wait_gradient, 0)
     gram = jnp.zeros((crew, ensemble), jnp.float32)
     piece = min(16, rows)
+    tiles = rows // SUB
     for first in range(0, rows, piece):
-        held = [owned[pl.ds(row, crew, stride=rows)] for row in range(first, first + piece)]
+        held = [
+            owned[pl.ds(row % tiles * SUB + row // tiles, crew, stride=rows)]
+            for row in range(first, first + piece)
+        ]
         gram = gram + lax.dot_general(
             jnp.concatenate(held, axis=1),
             spread[:, first * depth : (first + piece) * depth],
@@ -328,35 +331,37 @@
     mixing = -(step_size / ensemble) * gram + math.sqrt(2.0 * step_size / ensemble) * noise[
         pl.ds(first_column, crew)
     ]
-    for first in range(0, rows, piece):
-        cells = slice(first * depth, (first + piece) * depth)
-        result = (
-            centre[:, cells]
-            + 1.25 * spread[pl.ds(first_column, crew), cells]
-            + lax.dot_general(
-                mixing, spread[:, cells], (((1,), (0,)), ((), ())),
-                precision=lax.Precision.HIGHEST, preferred_element_type=jnp.float32,
-            )
-        )
-        for row in range(piece):
+    moved_block = moved.reshape(crew, rows, depth)
+
+    def result_part(to, first):
+        return (
+            moved_block.at[pl.ds(to * particles, particles), pl.ds(first, part)],
+            moved_out.at[:, pl.ds(place * rows + first, part)],
+        )
+
+    def result_copy(step, first):
+        to = lax.rem(place + step, team)
+        at = first // part
+        return remote(
+            *result_part(to, first), result_send.at[at, step - 1], result_recv.at[at, step - 1],
+            base + to, slab,
+        )
+
+    part = rows // 2
+    own_results = []
+    for first in range(0, rows, part):
+        cells = slice(first * depth, (first + part) * depth)
+        result = lax.dot_general(
+            mixing, spread[:, cells], (((1,), (0,)), ((), ())),
+            precision=lax.Precision.HIGHEST, preferred_element_type=jnp.float32,
+        ) - 0.25 * centre[:, cells]
+        for row in range(part):
             moved[pl.ds(first + row, crew, stride=rows)] = result[:, row * depth : (row + 1) * depth]
-
-    def result_copy(step):
-        to = lax.rem(place + step, team)
-        return remote(
-            moved_rows(to), moved_out.at[:, pl.ds(place * rows, rows)],
-            result_send.at[step - 1], result_recv.at[step - 1], base + to, slab,
-        )
-
-    def moved_rows(to):
-        return moved.reshape(crew, rows, depth).at[pl.ds(to * particles, particles)]
-
-    for step in range(1, team):
-        result_copy(step).start()
-    own_result = pltpu.make_async_copy(
-        moved_rows(place), moved_out.at[:, pl.ds(place * rows, rows)], own_sem.at[4]
-    )
-    own_result.start()
+        for step in range(1, team):
+            result_copy(step, first).start()
+        copy = pltpu.make_async_copy(*result_part(place, first), own_sem.at[6 + first // part])
+        copy.start()
+        own_results.append(copy)
 
     for step in order:
         slab_copy(step).wait_send()
@@ -364,20 +369,18 @@
         for copy in sides[which]:
             copy.wait_send()
 
-    def sent_member(step, carry):
-        member_copy(step).wait_send()
-        return carry
-
     def sent_crew(step, carry):
         gradient_copy(step).wait_send()
         part_copy(step).wait_send()
         return carry
 
-    lax.fori_loop(1, doms, sent_member, 0)
+    each_member(lambda copy: copy.wait_send())
     lax.fori_loop(1, crew, sent_crew, 0)
-    own_result.wait()
-    for step in range(1, team):
-        result_copy(step).wait()
+    for copy in own_results:
+        copy.wait()
+    for first in range(0, rows, part):
+        for step in range(1, team):
+            result_copy(step, first).wait()
 
 
 def on_device(logperm, source, observed, brownian):
@@ -389,9 +392,9 @@
     dma = pltpu.SemaphoreType.DMA
     scratch = [
         pltpu.VMEM((ensemble, ensemble), f32),
-        pltpu.VMEM((layers, rows, depth), f32),
-        pltpu.VMEM((layers, rows, depth), f32),
-        pltpu.VMEM((layers, rows, depth), f32),
+        pltpu.VMEM((layers * rows, depth), f32),
+        pltpu.VMEM((layers * rows, depth), f32),
+        pltpu.VMEM((layers * rows, depth), f32),
         pltpu.VMEM((layers, rows, depth), f32),
         pltpu.VMEM((ensemble, rows, depth), f32),
         pltpu.VMEM((ensemble, rows * depth), f32),
@@ -402,15 +405,15 @@
         pltpu.VMEM((ensemble, ensemble), f32),
         dma((slabs - 1,)), dma((slabs - 1,)),
         dma((2, 3)), dma((2, 3)),
-        dma((doms - 1,)), dma((doms - 1,)),
-        dma((6,)),
+        dma((doms,)), dma((doms,)),
+        dma((8,)),
         dma((crew - 1,)), dma((crew - 1,)),
         dma((crew - 1,)), dma((crew - 1,)),
-        dma((width - 1,)), dma((width - 1,)),
+        dma((2, width - 1)), dma((2, width - 1)),
         *scratch_fields(layers, rows, depth),
     ]
     far = pl.BlockSpec(memory_space=pltpu.HBM)
-    moved = pl.pallas_call(
+    drift = pl.pallas_call(
         fused_kernel,
         out_shape=jax.ShapeDtypeStruct((particles, width * rows, depth), f32),
         in_specs=[far] * 4,
@@ -424,7 +427,7 @@
         ),
         name="langevin",
     )(logperm, source, observed, brownian)
-    return moved.reshape(logperm.shape)
+    return 1.25 * logperm + drift.reshape(logperm.shape)
 
 
 def solution(mesh):

time: 50.8 us -> 50 us (0.984)
  the two profiles are of different devices: /device:TPU:17 before, /device:TPU:0 now
where the time goes in v4:
time: 50 us; the launch traced here: 49.9 us
  Pallas kernels  47.8 us (96%)
  other arithmetic  2.06 us (4%)
    pallas_call x1, Pallas kernels, on_device(): pl.pallas_call(fused_kernel, out_shape=jax.ShapeDtypeStruct((particles, w...  47.8 us
    add x1, other arithmetic, on_device(): return 1.25 * logperm + drift.reshape(logperm.shape)  2.06 us

profile of v4, /device:TPU:0, one launch (start us, length us, event | category | flops | bytes accessed | tf_op | source)
XLA Modules:
  0.0 49.9 jit_solution(12553314558579128919)
XLA Ops:
  0.0 47.8 %langevin.1 = f32[4,256,128]{2,1,0:T(8,128)} custom-call(f32[4,4,64,128]{3,2,1,0:T(8,128)} %logperm.1, f32[4,64,128]{2,1,0:T(8,128)} %source.1, f32[4,64,128]{2,1,0:T(8,128)} %observed.1, f32[32,32]{1,0:T(8,128)} %brownian_far.1), custom_call_target="tpu_custom_call" | custom-call | flops 39321600 | bytes 2097152 | tf_op jit(solution)/shard_map/langevin/pallas_call | solution.py:416
  47.8 2.1 %multiply_add_fusion = f32[4,4,64,128]{3,2,1,0:T(8,128)} fusion(f32[4,4,64,128]{3,2,1,0:T(8,128)} %bitcast.1, f32[4,4,64,128]{3,2,1,0:T(8,128)} %logperm.1), kind=kLoop, calls=%fused_computation | loop fusion | flops 262144 | bytes 1572864 | tf_op jit(solution)/shard_map/add | solution.py:430

commit v5 on v4

--- a/solution.py
+++ b/solution.py
@@ -125,6 +125,21 @@
     for side in range(1, 6):
         total = total + e_near[side] * (p_core - p_near[side]) * (q_core - q_near[side])
     return -0.5 * e_core * total
+
+
+def product(left, right, along):
+    def halves(value):
+        high = value.astype(jnp.bfloat16)
+        return high, (value - high.astype(jnp.float32)).astype(jnp.bfloat16)
+
+    def dot(a, b):
+        return lax.dot_general(a, b, (((1,), (along,)), ((), ())), preferred_element_type=jnp.float32)
+
+    left_high, left_low = halves(left)
+    right_high, right_low = halves(right)
+    both = dot(jnp.concatenate([left_high, left_low], axis=0), right_high)
+    count = left.shape[0]
+    return both[:count] + both[count:] + dot(left_high, right_low)
 
 
 def fused_kernel(
@@ -190,8 +205,13 @@
         )
 
     order = [2, 1, 3]
-    for step in order:
-        slab_copy(step).start()
+
+    def slab_piece(step, layer):
+        near = lax.rem(slab + step, slabs)
+        return remote(
+            logperm.at[near, layer], whole_blocks.at[slab * width + layer],
+            slab_send.at[step - 1], slab_recv.at[step - 1], dom, near,
+        )
 
     across = lax.rem(slab + 2, slabs)
     beside = slab + 1 - 2 * lax.rem(slab, 2)
@@ -212,9 +232,6 @@
         copy = pltpu.make_async_copy(block, full.reshape(layers, rows, depth).at[pl.ds(slab * width, width)], own_sem.at[1 + which])
         copy.start()
         local.append(copy)
-    sides[0][0].start()
-    sides[0][1].start()
-
     def member_copy(step):
         target = lax.rem(base + team * (1 + step // team), doms) + lax.rem(place + step, team)
         return remote(
@@ -222,22 +239,45 @@
             member_send.at[step], member_recv.at[step], target, slab,
         )
 
-    def each_member(act):
+    def each_member(act, first, last):
         def body(step, carry):
             act(member_copy(step))
             return carry
 
-        lax.fori_loop(0, doms - team, body, 0)
-        lax.fori_loop(doms - team + 1, doms, body, 0)
-
-    each_member(lambda copy: copy.start())
+        lax.fori_loop(first, last, body, 0)
+
+    def member_piece(step, particle):
+        target = lax.rem(base + team * (1 + step // team), doms) + lax.rem(place + step, team)
+        return remote(
+            logperm.at[particle, lax.rem(target, team)], members.at[dom * particles + particle],
+            member_send.at[step], member_recv.at[step], target, slab,
+        )
+
+    for piece in range(width):
+        for step in order:
+            slab_piece(step, piece).start()
+        for step in range(min(team, doms - team)):
+            member_piece(step, piece).start()
+    sides[0][0].start()
+    sides[0][1].start()
+
+    def start_rest(step, carry):
+        member_copy(step).start()
+        return carry
+
+    lax.fori_loop(doms - team + 1, doms, start_rest, 0)
+    lax.fori_loop(min(team, doms - team), doms - team, start_rest, 0)
     own_members = pltpu.make_async_copy(
         logperm.at[:, place], members.at[pl.ds(dom * particles, particles)], own_sem.at[3]
     )
     own_members.start()
 
     fetch.wait()
-    noise[...] = brownian[...].T
+    turned = [
+        brownian[pl.ds(pl.multiple_of(lax.rem(base + at * team, doms) * particles, 8), crew)]
+        for at in range(doms // team)
+    ]
+    noise[...] = jnp.concatenate(turned, axis=0).T
     own_block.wait()
     for step in order:
         slab_copy(step).wait_recv()
@@ -278,36 +318,49 @@
     lax.fori_loop(1, layers, send_gradient, 0, unroll=5)
     owned[pl.ds(column * rows, rows)] = gradient_layer(mine, fields)
 
+    member_rows = members.reshape(ensemble * rows, depth)
+    tiles = rows // SUB
+
+    def line(team_at, row):
+        first = lax.rem(base + team_at * team, doms) * particles
+        return member_rows[pl.ds(first * rows + row, crew, stride=rows)]
+
     own_members.wait()
-    each_member(lambda copy: copy.wait_recv())
-    member_rows = members.reshape(ensemble * rows, depth)
+    each_member(lambda copy: copy.wait_recv(), doms - team + 1, doms)
     for row in range(rows):
-        across_cells = member_rows[pl.ds(row, ensemble, stride=rows)]
-        mean = jnp.sum(across_cells, axis=0, keepdims=True) * (1.0 / ensemble)
-        spread[:, row * depth : (row + 1) * depth] = across_cells - mean
-        centre[:, row * depth : (row + 1) * depth] = mean
+        cells = slice(row * depth, (row + 1) * depth)
+        values = line(0, row)
+        mean = jnp.sum(values, axis=0, keepdims=True) * (1.0 / crew)
+        spread[0:crew, cells] = values - mean
+        centre[:, cells] = mean
 
     def wait_gradient(step, carry):
         gradient_copy(step).wait_recv()
         return carry
 
     lax.fori_loop(1, crew, wait_gradient, 0)
-    gram = jnp.zeros((crew, ensemble), jnp.float32)
     piece = min(16, rows)
-    tiles = rows // SUB
-    for first in range(0, rows, piece):
-        held = [
-            owned[pl.ds(row % tiles * SUB + row // tiles, crew, stride=rows)]
-            for row in range(first, first + piece)
-        ]
-        gram = gram + lax.dot_general(
-            jnp.concatenate(held, axis=1),
-            spread[:, first * depth : (first + piece) * depth],
-            (((1,), (1,)), ((), ())),
-            precision=lax.Precision.HIGHEST,
-            preferred_element_type=jnp.float32,
-        )
-    parts[mine] = gram
+
+    def held(first):
+        return jnp.concatenate(
+            [
+                owned[pl.ds((row % tiles) * SUB + row // tiles, crew, stride=rows)]
+                for row in range(first, first + piece)
+            ],
+            axis=1,
+        )
+
+    for team_at in range(doms // team):
+        at = slice(team_at * crew, (team_at + 1) * crew)
+        if team_at > 0:
+            each_member(lambda copy: copy.wait_recv(), (team_at - 1) * team, team_at * team)
+            for row in range(rows):
+                cells = slice(row * depth, (row + 1) * depth)
+                spread[at, cells] = line(team_at, row) - centre[:, cells]
+        gram = jnp.zeros((crew, crew), jnp.float32)
+        for first in range(0, rows, piece):
+            gram = gram + product(held(first), spread[at, first * depth : (first + piece) * depth], 1)
+        parts[mine, :, at] = gram
 
     def part_copy(step):
         _, at_dom, at_slab = crew_device(step)
@@ -326,11 +379,13 @@
     lax.fori_loop(1, crew, start_part, 0)
     lax.fori_loop(1, crew, wait_part, 0)
     gram = jnp.sum(parts[...], axis=0)
+    gram = gram - jnp.sum(gram, axis=1, keepdims=True) * (1.0 / ensemble)
     step_size = ensemble / (4.0 * (layers * rows * depth + 1))
     first_column = pl.multiple_of(base * particles, 8)
     mixing = -(step_size / ensemble) * gram + math.sqrt(2.0 * step_size / ensemble) * noise[
         pl.ds(first_column, crew)
     ]
+    mixing = mixing - (jnp.sum(mixing, axis=1, keepdims=True) + 0.25) * (1.0 / ensemble)
     moved_block = moved.reshape(crew, rows, depth)
 
     def result_part(to, first):
@@ -351,10 +406,7 @@
     own_results = []
     for first in range(0, rows, part):
         cells = slice(first * depth, (first + part) * depth)
-        result = lax.dot_general(
-            mixing, spread[:, cells], (((1,), (0,)), ((), ())),
-            precision=lax.Precision.HIGHEST, preferred_element_type=jnp.float32,
-        ) - 0.25 * centre[:, cells]
+        result = spread[0:crew, cells] * 1.25 + centre[:, cells] + product(mixing, spread[:, cells], 0)
         for row in range(part):
             moved[pl.ds(first + row, crew, stride=rows)] = result[:, row * depth : (row + 1) * depth]
         for step in range(1, team):
@@ -374,7 +426,8 @@
         part_copy(step).wait_send()
         return carry
 
-    each_member(lambda copy: copy.wait_send())
+    each_member(lambda copy: copy.wait_send(), 0, doms - team)
+    each_member(lambda copy: copy.wait_send(), doms - team + 1, doms)
     lax.fori_loop(1, crew, sent_crew, 0)
     for copy in own_results:
         copy.wait()
@@ -413,7 +466,7 @@
         *scratch_fields(layers, rows, depth),
     ]
     far = pl.BlockSpec(memory_space=pltpu.HBM)
-    drift = pl.pallas_call(
+    moved = pl.pallas_call(
         fused_kernel,
         out_shape=jax.ShapeDtypeStruct((particles, width * rows, depth), f32),
         in_specs=[far] * 4,
@@ -427,7 +480,7 @@
         ),
         name="langevin",
     )(logperm, source, observed, brownian)
-    return 1.25 * logperm + drift.reshape(logperm.shape)
+    return moved.reshape(logperm.shape)
 
 
 def solution(mesh):

time: 50 us -> 49.9 us (level)
  other arithmetic: 2.06 us -> 0 us
  local copies, waits for them, and re-layouts: 0 us -> 1.89 us
    add x1 -> x0, other arithmetic: 2.06 us -> none  [on_device(): return 1.25 * logperm + drift.reshape(logperm.shape)]
    unnamed x0 -> x1, local copies, waits for them, and re-layouts: none -> 1.89 us
where the time goes in v5:
time: 49.9 us; the launch traced here: 49.7 us
  Pallas kernels  47.8 us (96%)
  local copies, waits for them, and re-layouts  1.89 us (4%)
    pallas_call x1, Pallas kernels, on_device(): pl.pallas_call(fused_kernel, out_shape=jax.ShapeDtypeStruct((particles, w...  47.8 us
    unnamed x1, local copies, waits for them, and re-layouts  1.89 us

profile of v5, /device:TPU:0, one launch (start us, length us, event | category | flops | bytes accessed | tf_op | source)
XLA Modules:
  0.0 49.7 jit_solution(12753086292720041006)
XLA Ops:
  0.0 47.8 %langevin.1 = f32[4,256,128]{2,1,0:T(8,128)} custom-call(f32[4,4,64,128]{3,2,1,0:T(8,128)} %logperm.1, f32[4,64,128]{2,1,0:T(8,128)} %source.1, f32[4,64,128]{2,1,0:T(8,128)} %observed.1, f32[32,32]{1,0:T(8,128)} %brownian_far.1), custom_call_target="tpu_custom_call" | custom-call | flops 39321600 | bytes 2097152 | tf_op jit(solution)/shard_map/langevin/pallas_call | solution.py:469
  47.9 1.9 %copy.6 = f32[4,4,64,128]{3,2,1,0:T(8,128)} copy(f32[4,4,64,128]{3,2,1,0:T(8,128)} %bitcast.1) | data formatting | bytes 1048576

commit v6 on v5

--- a/solution.py
+++ b/solution.py
@@ -37,6 +37,19 @@
     return core, (ref[layer], ref[layer + 2], *joined)
 
 
+def plane_sum(core, masks):
+    rows, depth = core.shape
+    before = jnp.concatenate(
+        [jnp.where(masks[2], 0.0, pltpu.roll(core[rows - SUB :], 1, 0)), core[: rows - SUB]], axis=0
+    )
+    after = jnp.concatenate(
+        [core[SUB:], jnp.where(masks[3], 0.0, pltpu.roll(core[:SUB], SUB - 1, 0))], axis=0
+    )
+    left = jnp.where(masks[4], 0.0, pltpu.roll(core, 1, 1))
+    right = jnp.where(masks[5], 0.0, pltpu.roll(core, depth - 1, 1))
+    return (before + after) + (left + right)
+
+
 def border(ref, layers, rows, depth, fill):
     ref[0] = jnp.full((rows, depth), fill, jnp.float32)
     ref[layers + 1] = jnp.full((rows, depth), fill, jnp.float32)
@@ -75,10 +88,12 @@
     lax.fori_loop(0, layers, divide, 0, unroll=8)
 
 
-def relax(rhs, ping, pong, fields):
+def relax(rhs, ping, pong, fields, between):
     e, inverse, gain, start = fields[0], fields[4], fields[5], fields[6]
     layers, rows, depth = inverse.shape
     masks = edge_masks(depth)
+    lane = lax.broadcasted_iota(jnp.int32, (rows, depth), 1)
+    masks = (*masks, lane == 0, lane == depth - 1)
 
     def first(layer, carry):
         value = inverse[layer] * rhs(layer)
@@ -88,30 +103,28 @@
 
     lax.fori_loop(0, layers, first, 0, unroll=8)
 
-    def swept(old, layer):
-        _, near = neighbors(old, layer, masks, 0.0)
-        total = (near[0] + near[1]) + (near[2] + near[3]) + (near[4] + near[5])
-        return start[layer] + gain[layer] * total
-
-    def sweep(old, new):
-        def one(layer, carry):
-            new[layer + 1] = swept(old, layer)
-            return carry
-
-        lax.fori_loop(0, layers, one, 0, unroll=layers)
+    def sweep(old, new, finish):
+        below, core = None, old[1]
+        for layer in range(layers):
+            above = old[layer + 2] if layer + 1 < layers else None
+            total = plane_sum(core, masks)
+            if below is not None:
+                total = total + below
+            if above is not None:
+                total = total + above
+            new[layer + 1] = finish(layer, start[layer] + gain[layer] * total)
+            below, core = core, above
 
     def pair(index, carry):
-        sweep(ping, pong)
-        sweep(pong, ping)
-        return carry
-
-    lax.fori_loop(0, (SWEEPS - 2) // 2, pair, 0)
-
-    def last(layer, carry):
-        pong[layer + 1] = swept(ping, layer) / e[layer + 1]
-        return carry
-
-    lax.fori_loop(0, layers, last, 0, unroll=layers)
+        sweep(ping, pong, lambda layer, value: value)
+        sweep(pong, ping, lambda layer, value: value)
+        return carry
+
+    pairs = (SWEEPS - 2) // 2
+    lax.fori_loop(0, pairs - 1, pair, 0)
+    between()
+    lax.fori_loop(pairs - 1, pairs, pair, 0)
+    sweep(ping, pong, lambda layer, value: value / e[layer + 1])
 
 
 def gradient_layer(layer, fields):
@@ -206,12 +219,8 @@
 
     order = [2, 1, 3]
 
-    def slab_piece(step, layer):
-        near = lax.rem(slab + step, slabs)
-        return remote(
-            logperm.at[near, layer], whole_blocks.at[slab * width + layer],
-            slab_send.at[step - 1], slab_recv.at[step - 1], dom, near,
-        )
+    for step in order:
+        slab_copy(step).start()
 
     across = lax.rem(slab + 2, slabs)
     beside = slab + 1 - 2 * lax.rem(slab, 2)
@@ -232,6 +241,9 @@
         copy = pltpu.make_async_copy(block, full.reshape(layers, rows, depth).at[pl.ds(slab * width, width)], own_sem.at[1 + which])
         copy.start()
         local.append(copy)
+    sides[0][0].start()
+    sides[0][1].start()
+
     def member_copy(step):
         target = lax.rem(base + team * (1 + step // team), doms) + lax.rem(place + step, team)
         return remote(
@@ -246,27 +258,12 @@
 
         lax.fori_loop(first, last, body, 0)
 
-    def member_piece(step, particle):
-        target = lax.rem(base + team * (1 + step // team), doms) + lax.rem(place + step, team)
-        return remote(
-            logperm.at[particle, lax.rem(target, team)], members.at[dom * particles + particle],
-            member_send.at[step], member_recv.at[step], target, slab,
-        )
-
-    for piece in range(width):
-        for step in order:
-            slab_piece(step, piece).start()
-        for step in range(min(team, doms - team)):
-            member_piece(step, piece).start()
-    sides[0][0].start()
-    sides[0][1].start()
-
-    def start_rest(step, carry):
+    def start_member(step, carry):
         member_copy(step).start()
         return carry
 
-    lax.fori_loop(doms - team + 1, doms, start_rest, 0)
-    lax.fori_loop(min(team, doms - team), doms - team, start_rest, 0)
+    lax.fori_loop(0, doms - team, start_member, 0)
+    lax.fori_loop(doms - team + 1, doms, start_member, 0)
     own_members = pltpu.make_async_copy(
         logperm.at[:, place], members.at[pl.ds(dom * particles, particles)], own_sem.at[3]
     )
@@ -289,10 +286,13 @@
     sides[0][1].wait_recv()
     local[0].wait()
     sides[0][2].wait_recv()
-    relax(lambda layer: interleaved(full_source, layer, rows), fields[1], fields[2], fields)
+
+    def forward_observed():
+        sides[1][0].wait_recv()
+        sides[1][2].start()
+
+    relax(lambda layer: interleaved(full_source, layer, rows), fields[1], fields[2], fields, forward_observed)
     pressure = fields[2]
-    sides[1][0].wait_recv()
-    sides[1][2].start()
     sides[1][1].wait_recv()
     local[1].wait()
     sides[1][2].wait_recv()
@@ -300,7 +300,7 @@
     def misfit(layer):
         return misfit_weight * (pressure[layer + 1] - interleaved(full_observed, layer, rows))
 
-    relax(misfit, fields[1], fields[3], fields)
+    relax(misfit, fields[1], fields[3], fields, lambda: None)
 
     def gradient_copy(step):
         layer, at_dom, at_slab = crew_device(step)

time: 49.9 us -> 49.8 us (level)
  no operation moved by 1% of the time
where the time goes in v6:
time: 49.8 us; the launch traced here: 49.7 us
  Pallas kernels  47.8 us (96%)
  local copies, waits for them, and re-layouts  1.89 us (4%)
    pallas_call x1, Pallas kernels, on_device(): pl.pallas_call(fused_kernel, out_shape=jax.ShapeDtypeStruct((particles, w...  47.8 us
    unnamed x1, local copies, waits for them, and re-layouts  1.89 us

profile of v6, /device:TPU:0, one launch (start us, length us, event | category | flops | bytes accessed | tf_op | source)
XLA Modules:
  0.0 49.7 jit_solution(8139485204155801677)
XLA Ops:
  0.0 47.8 %langevin.1 = f32[4,256,128]{2,1,0:T(8,128)} custom-call(f32[4,4,64,128]{3,2,1,0:T(8,128)} %logperm.1, f32[4,64,128]{2,1,0:T(8,128)} %source.1, f32[4,64,128]{2,1,0:T(8,128)} %observed.1, f32[32,32]{1,0:T(8,128)} %brownian_far.1), custom_call_target="tpu_custom_call" | custom-call | flops 39321600 | bytes 2097152 | tf_op jit(solution)/shard_map/langevin/pallas_call | solution.py:469
  47.8 1.9 %copy.6 = f32[4,4,64,128]{3,2,1,0:T(8,128)} copy(f32[4,4,64,128]{3,2,1,0:T(8,128)} %bitcast.1) | data formatting | bytes 1048576

commit v7 on v6

--- a/solution.py
+++ b/solution.py
@@ -434,6 +434,18 @@
     for first in range(0, rows, part):
         for step in range(1, team):
             result_copy(step, first).wait()
+
+
+def hand_over(moved, out, sems):
+    copies = [
+        pltpu.make_async_copy(moved.at[particle, layer], out.at[particle, layer], sems.at[particle, layer])
+        for particle in range(moved.shape[0])
+        for layer in range(moved.shape[1])
+    ]
+    for copy in copies:
+        copy.start()
+    for copy in copies:
+        copy.wait()
 
 
 def on_device(logperm, source, observed, brownian):
@@ -480,7 +492,14 @@
         ),
         name="langevin",
     )(logperm, source, observed, brownian)
-    return moved.reshape(logperm.shape)
+    return pl.pallas_call(
+        hand_over,
+        out_shape=jax.ShapeDtypeStruct(logperm.shape, f32),
+        in_specs=[far],
+        out_specs=far,
+        scratch_shapes=[dma((particles, width))],
+        name="hand_over",
+    )(moved.reshape(logperm.shape))
 
 
 def solution(mesh):

time: 49.8 us -> 65.1 us (1.31)
  Pallas kernels: 47.8 us -> 64.9 us
  local copies, waits for them, and re-layouts: 1.89 us -> 0 us
    pallas_call x0 -> x1, Pallas kernels: none -> 17.1 us  [on_device(): pl.pallas_call(hand_over, out_shape=jax.ShapeDtypeStruct(logperm.shape, f...]
    unnamed x1 -> x0, local copies, waits for them, and re-layouts: 1.89 us -> none
where the time goes in v7:
time: 65.1 us; the launch traced here: 64.9 us
  Pallas kernels  64.9 us (100%)
    pallas_call x1, Pallas kernels, on_device(): pl.pallas_call(fused_kernel, out_shape=jax.ShapeDtypeStruct((particles, w...  47.8 us
    pallas_call x1, Pallas kernels, on_device(): pl.pallas_call(hand_over, out_shape=jax.ShapeDtypeStruct(logperm.shape, f...  17.1 us

profile of v7, /device:TPU:0, one launch (start us, length us, event | category | flops | bytes accessed | tf_op | source)
XLA Modules:
  0.0 64.9 jit_solution(9304823290216152620)
XLA Ops:
  0.0 47.8 %langevin.1 = f32[4,256,128]{2,1,0:T(8,128)} custom-call(f32[4,4,64,128]{3,2,1,0:T(8,128)} %logperm.1, f32[4,64,128]{2,1,0:T(8,128)} %source.1, f32[4,64,128]{2,1,0:T(8,128)} %observed.1, f32[32,32]{1,0:T(8,128)} %brownian_far.1), custom_call_target="tpu_custom_call" | custom-call | flops 39321600 | bytes 2097152 | tf_op jit(solution)/shard_map/langevin/pallas_call | solution.py:481
  47.8 17.1 %hand_over.1 = f32[4,4,64,128]{3,2,1,0:T(8,128)} custom-call(f32[4,4,64,128]{3,2,1,0:T(8,128)} %bitcast.1), custom_call_target="tpu_custom_call" | custom-call | tf_op jit(solution)/shard_map/hand_over/pallas_call | solution.py:495
